TPU v7x, 256 devices: a whole 4x4x8 slice. The times are simulated.
256 devices in a mesh: src: 16 (over y, x_lo, core), dst: 16 (over z, x_hi).
Axes of the slice: x: 4 (x_hi: 2, x_lo: 2; x = x_hi * 2 + x_lo), y: 4, z: 8, core: 2. Of those that a mesh axis runs over, the one named last changes fastest.
Arguments:
- raw: bfloat16 [32768, 256], P(('src', 'dst')), may hold values from -6 to 6
- enc_w1: bfloat16 [256, 512], replicated, may hold values from -0.375 to 0.375
- enc_w2: bfloat16 [512, 256], replicated, may hold values from -0.25 to 0.25
- block_weights: float32 [32768, 128, 128], P(('src', 'dst')), may hold values from -0.046875 to 0.046875
- block_cols: int32 [32768], P(('src', 'dst')), may hold values from 0 to 15, as said below
- noise: bfloat16 [3, 32768, 256], P(None, ('src', 'dst')), may hold values from -3 to 3
Outputs:
- encoded: bfloat16 [32768, 256], P(('src', 'dst'))
- hops: bfloat16 [3, 32768, 256], P(None, ('src', 'dst'))
Inputs may be any that keep to these rules, and one draw needn't show every extreme that they name: `block_cols`: entry b of each device's 128 entries belongs to row block b // 8; row blocks 2j and 2j+1 of a device together name every column block exactly once, each naming 16 // 2 distinct ones.
All inputs are finite; a program needn't handle non-finite values.
Results may differ from a plain program's by a relative error of at most 0.0058.
Values may be sent and summed in bfloat16 or wider, within the bound.
No kernel may reach another device: no remote copies, remote signals or barrier semaphores. Data moves between devices by JAX's collectives and lax.ppermute only.
A program may use at most 128 MiB of HBM per device.

v0:
```python
import functools

import jax
import jax.numpy as jnp
from jax import lax
from jax.experimental import pallas as pl
from jax.experimental.pallas import tpu as pltpu
from jax.sharding import PartitionSpec as P

HOPS = 3
BS = 128
BF = jnp.bfloat16
F32 = jnp.float32

NY, NX, NZ = 4, 2, 8
YX_GROUPS = [[2 * i + c for i in range(NY * NX)] for c in range(2)]
ARRIVAL = [
    (o, f)
    for f, offsets in (
        (0, (0, 3, -2)),
        (1, (0, 3, -2)),
        (0, (-1, 2, -3)),
        (0, (1, 4)),
        (1, (-1, 2, -3)),
        (1, (1, 4)),
    )
    for o in offsets
]


def shift_dst(x, dz, flip=0):
    perm = [(i, ((i // 2 + dz) % NZ) * 2 + ((i % 2) ^ flip)) for i in range(NZ * 2)]
    return lax.ppermute(x, "dst", perm)


def swap_core(x):
    return lax.ppermute(x, "src", [(i, i ^ 1) for i in range(NY * NX * 2)])


def normalize_rows(z):
    return (z * lax.rsqrt(jnp.mean(z * z, axis=-1, keepdims=True) + 1e-06)).astype(BF)


SLOTS = {
    f: sum(k << (4 * (o % NZ)) for k, (o, g) in enumerate(ARRIVAL) if g == f) for f in (0, 1)
}


def as_int32(v):
    return v - 2**32 if v >= 2**31 else v


def pack_kernel(other, info_ref, w_ref, *refs):
    n = (len(refs) - 1) // 2
    passed, o_ref, passed_out = refs[:n], refs[n], refs[n + 1 :]
    p = pl.program_id(0)
    core, z, xh = info_ref[0], info_ref[1], info_ref[2]

    @pl.when(p == 0)
    def _():
        for i, o in zip(passed, passed_out):
            o[...] = i[...]

    row = pl.multiple_of(p * BS, BS)
    first = 3 + (2 * p + ((core ^ other) & 1)) * 8
    o_ref[pl.ds(row, BS), :] = jnp.zeros((BS, o_ref.shape[1]), BF)
    for j in range(8):
        col = info_ref[first + j]
        table = jnp.where(
            (col & 1) == xh, jnp.int32(as_int32(SLOTS[0])), jnp.int32(as_int32(SLOTS[1]))
        )
        shift = (((col >> 1) - z) & (NZ - 1)) * 4
        at = pl.multiple_of(((table >> shift) & 15) * BS, BS)
        o_ref[pl.ds(row, BS), pl.ds(at, BS)] = w_ref[0, 0, j].astype(BF)


def pack(weights, info, other, *passed):
    pairs = weights.shape[0] // 16
    blocks = weights.reshape(pairs, 2, 8, BS, BS)
    whole = pl.BlockSpec(memory_space=pltpu.VMEM)
    return pl.pallas_call(
        functools.partial(pack_kernel, other),
        out_shape=[jax.ShapeDtypeStruct((pairs * BS, 16 * BS), BF)]
        + [jax.ShapeDtypeStruct(x.shape, x.dtype) for x in passed],
        grid_spec=pltpu.PrefetchScalarGridSpec(
            num_scalar_prefetch=1,
            grid=(pairs,),
            in_specs=[
                pl.BlockSpec((1, 1, 8, BS, BS), lambda p, i: (p, (i[0] ^ other) & 1, 0, 0, 0))
            ]
            + [whole] * len(passed),
            out_specs=[whole] * (1 + len(passed)),
        ),
        cost_estimate=pl.CostEstimate(flops=0, bytes_accessed=6 * 2**20, transcendentals=0),
        compiler_params=pltpu.CompilerParams(vmem_limit_bytes=16 * 2**20),
        name="pack",
    )(info, blocks, *passed)


def far_phase(h):
    return shift_dst(h, -3), shift_dst(h, 2)


def gather_dst(h, low, high):
    g = jnp.concatenate([h, low, high])
    x = shift_dst(g, 0, 1)
    up, down = shift_dst(g, 1), shift_dst(g[: 2 * BS], -1)
    early = jnp.concatenate([g, x, up, down])
    late = jnp.concatenate([shift_dst(x, 1), shift_dst(x[: 2 * BS], -1)])
    return early, late


def shards(raw, enc_w1, enc_w2, block_weights, block_cols, noise):
    hidden = jax.nn.silu(jnp.dot(raw, enc_w1, preferred_element_type=F32)).astype(BF)
    encoded = normalize_rows(jnp.dot(hidden, enc_w2, preferred_element_type=F32))

    s, d = lax.axis_index("src"), lax.axis_index("dst")
    info = jnp.concatenate([jnp.stack([s % 2, d // 2, d % 2]).astype(jnp.int32), block_cols])
    low, high = far_phase(encoded)
    other_rows, own = pack(block_weights, info, 1, encoded)
    (own_rows,) = pack(block_weights, info, 0)

    kept = []
    for step in range(HOPS):
        near, rest = gather_dst(own, low, high)
        n = near.shape[0]

        def early(a):
            return lax.optimization_barrier(
                jnp.dot(a[:, :n], near, preferred_element_type=F32)
            )

        def late(a):
            return jnp.dot(a[:, n:], rest, preferred_element_type=F32)

        early_other, early_own = early(other_rows), early(own_rows)
        other = swap_core((early_other + late(other_rows)).astype(BF))
        mine = early_own + late(own_rows) + other.astype(F32)
        parts = lax.all_to_all(
            mine.astype(BF).reshape(NY * NX, BS, -1), "src", 0, 0, axis_index_groups=YX_GROUPS
        )
        total = parts.astype(F32).sum(axis=0) + noise[step].astype(F32)
        own = normalize_rows(total)
        kept.append(own)
        if step < HOPS - 1:
            low, high = far_phase(own)
    return (encoded, jnp.stack(kept))


def solution(mesh):
    placed = (
        P(("src", "dst"), None),
        P(),
        P(),
        P(("src", "dst"), None, None),
        P(("src", "dst")),
        P(None, ("src", "dst"), None),
    )
    return jax.shard_map(
        shards,
        mesh=mesh,
        in_specs=placed,
        out_specs=(P(("src", "dst"), None), P(None, ("src", "dst"), None)),
        check_vma=False,
    )
```

profile of v0, /device:TPU:1, one launch (start us, length us, event | category | flops | bytes accessed | tf_op | source)
XLA Modules:
  0.0 132.4 jit_solution(2855701734188319032)
XLA Ops:
  0.6 0.9 copy-done
  1.6 1.4 %multiply_reduce_fusion.2 = (f32[128]{0:T(128)S(1)}, f32[128,256]{1,0:T(8,128)S(1)}) fusion(bf16[512,256]{1,0:T(8,128)(2,1)S(1)} %copy-done, bf16[128,256]{1,0:T(8,128)(2,1)} %param.6, bf16[256,512]{1,0:T(8,128)(2,1)} %param.7), kind=kOutput, calls=%fused_computation.62 | convolution fusion | flops 67501952 | bytes 721408 | tf_op jit(solution)/shard_map/dot_general | solution.py:115
  3.1 7.4 %collective-permute-start = (bf16[128,256]{1,0:T(8,128)(2,1)S(1)}, bf16[128,256]{1,0:T(8,128)(2,1)S(1)}, u32[]{:S(2)}, u32[]{:S(2)}) collective-permute-start(bf16[128,256]{1,0:T(8,128)(2,1)S(1)} %multiply_convert_fusion.3.refs_0_), channel_id=1, source_target_pairs={{0,10},{1,11},{2,12},{3,13},{4,14},{5,15},{6,0},{7,1},{8,2},{9,3},... | collective-permute-start | bytes 196616 | tf_op jit(solution)/shard_map/ppermute | solution.py:33
  10.5 1.2 collective-permute-start.1
  11.7 0.7 pad_add_fusion.info_ref
  12.4 3.4 %copy-done.1 = f32[128,128,128]{2,1,0:T(8,128)S(1)} copy-done((f32[128,128,128]{2,1,0:T(8,128)S(1)}, f32[128,128,128]{2,1,0:T(8,128)}, u32[]{:S(2)}) %copy-start.1) | copy-done | bytes 8388632
  15.8 1.4 %pack.3 = (bf16[1024,2048]{1,0:T(8,128)(2,1)S(1)}, bf16[128,256]{1,0:T(8,128)(2,1)S(1)}) custom-call(s32[131]{0:T(256)S(1)} %pad_add_fusion.info_ref, f32[8,2,8,128,128]{4,3,2,1,0:T(8,128)S(1)} %bitcast.54, bf16[128,256]{1,0:T(8,128)(2,1)S(1)} %multiply_convert_fusion.3.refs_0_), custom_call_target="tpu_custom_call" | custom-call | bytes 6291456 | tf_op jit(solution)/shard_map/pack/pallas_call | solution.py:81
  17.3 2.8 %collective-permute-start.2 = (bf16[384,256]{1,0:T(8,128)(2,1)S(1)}, bf16[384,256]{1,0:T(8,128)(2,1)S(1)}, u32[]{:S(2)}, u32[]{:S(2)}) collective-permute-start(bf16[384,256]{1,0:T(8,128)(2,1)S(1)} %get-tuple-element.13), channel_id=1, source_target_pairs={{0,1},{1,0},{2,3},{3,2},{4,5},{5,4},{6,7},{7,6},{8,9},{9,8},{10,11... | collective-permute-start | bytes 589832 | tf_op jit(solution)/shard_map/ppermute | solution.py:33
  20.1 1.4 %pack.2 = bf16[1024,2048]{1,0:T(8,128)(2,1)S(1)} custom-call(s32[131]{0:T(256)S(1)} %pad_add_fusion.info_ref, f32[8,2,8,128,128]{4,3,2,1,0:T(8,128)S(1)} %bitcast.55), custom_call_target="tpu_custom_call" | custom-call | bytes 6291456 | tf_op jit(solution)/shard_map/pack/pallas_call | solution.py:81
  21.6 2.7 %collective-permute-start.4 = (bf16[256,256]{1,0:T(8,128)(2,1)S(1)}, bf16[256,256]{1,0:T(8,128)(2,1)S(1)}, u32[]{:S(2)}, u32[]{:S(2)}) collective-permute-start(bf16[256,256]{1,0:T(8,128)(2,1)S(1)} %pad_maximum_fusion.3), channel_id=1, source_target_pairs={{0,14},{1,15},{2,0},{3,1},{4,2},{5,3},{6,4},{7,5},{8,6},{9,7},{10,... | collective-permute-start | bytes 393224 | tf_op jit(solution)/shard_map/ppermute | solution.py:33
  24.4 1.7 %collective-permute-start.6 = (bf16[256,256]{1,0:T(8,128)(2,1)S(1)}, bf16[256,256]{1,0:T(8,128)(2,1)S(1)}, u32[]{:S(2)}, u32[]{:S(2)}) collective-permute-start(bf16[256,256]{1,0:T(8,128)(2,1)S(1)} %slice.56), channel_id=1, source_target_pairs={{0,14},{1,15},{2,0},{3,1},{4,2},{5,3},{6,4},{7,5},{8,6},{9,7},{10,... | collective-permute-start | bytes 393224 | tf_op jit(solution)/shard_map/ppermute | solution.py:33
  26.1 1.6 %collective-permute-done.3 = bf16[384,256]{1,0:T(8,128)(2,1)S(1)} collective-permute-done((bf16[384,256]{1,0:T(8,128)(2,1)S(1)}, bf16[384,256]{1,0:T(8,128)(2,1)S(1)}, u32[]{:S(2)}, u32[]{:S(2)}) %collective-permute-start.3) | collective-permute-done | bytes 196640 | tf_op jit(solution)/shard_map/ppermute | solution.py:33
  27.7 1.0 fusion.10
  28.7 3.1 %collective-permute-done.5 = bf16[384,256]{1,0:T(8,128)(2,1)S(1)} collective-permute-done((bf16[384,256]{1,0:T(8,128)(2,1)S(1)}, bf16[384,256]{1,0:T(8,128)(2,1)S(1)}, u32[]{:S(2)}, u32[]{:S(2)}) %collective-permute-start.5) | collective-permute-done | bytes 196640 | tf_op jit(solution)/shard_map/ppermute | solution.py:33
  31.9 0.6 fusion.22
  32.5 0.2 add_convert_fusion.5
  32.6 3.7 %collective-permute-start.7 = (bf16[1024,256]{1,0:T(8,128)(2,1)S(1)}, bf16[1024,256]{1,0:T(8,128)(2,1)S(1)}, u32[]{:S(2)}, u32[]{:S(2)}) collective-permute-start(bf16[1024,256]{1,0:T(8,128)(2,1)S(1)} %add_convert_fusion.5), channel_id=1, source_target_pairs={{0,16},{16,0},{32,48},{48,32},{64,80},{80,64},{96,112},{112,96},{1... | collective-permute-start | bytes 1572872 | tf_op jit(solution)/shard_map/ppermute | solution.py:37
  36.3 1.0 fusion.4
  37.3 0.6 fusion.16
  37.9 0.2 add_convert_fusion.4
  38.1 14.2 %all_to_all.15 = bf16[8,128,256]{2,1,0:T(8,128)(2,1)S(1)} all-to-all(bf16[8,128,256]{2,1,0:T(8,128)(2,1)S(1)} %bitcast.56), channel_id=1, replica_groups={{0,32,64,96,128,160,192,224},{16,48,80,112,144,176,208,240},{1,33,65,97..., dimensions={0} | all-to-all | bytes 1048576 | tf_op jit(solution)/shard_map/all_to_all | solution.py:139
  52.4 0.1 multiply_reduce_fusion.1
  52.5 0.1 constant_dynamic-update-slice_fusion.16
  52.7 1.6 %collective-permute-start.9 = (bf16[128,256]{1,0:T(8,128)(2,1)S(1)}, bf16[128,256]{1,0:T(8,128)(2,1)S(1)}, u32[]{:S(2)}, u32[]{:S(2)}) collective-permute-start(bf16[128,256]{1,0:T(8,128)(2,1)S(1)} %get-tuple-element.9), channel_id=1, source_target_pairs={{0,4},{1,5},{2,6},{3,7},{4,8},{5,9},{6,10},{7,11},{8,12},{9,13},{1... | collective-permute-start | bytes 196616 | tf_op jit(solution)/shard_map/ppermute | solution.py:33
  54.3 4.3 %collective-permute-done.8 = bf16[128,256]{1,0:T(8,128)(2,1)S(1)} collective-permute-done((bf16[128,256]{1,0:T(8,128)(2,1)S(1)}, bf16[128,256]{1,0:T(8,128)(2,1)S(1)}, u32[]{:S(2)}, u32[]{:S(2)}) %collective-permute-start.8) | collective-permute-done | bytes 65568 | tf_op jit(solution)/shard_map/ppermute | solution.py:33
  58.6 2.6 %collective-permute-start.10 = (bf16[384,256]{1,0:T(8,128)(2,1)S(1)}, bf16[384,256]{1,0:T(8,128)(2,1)S(1)}, u32[]{:S(2)}, u32[]{:S(2)}) collective-permute-start(bf16[384,256]{1,0:T(8,128)(2,1)S(1)} %pad_maximum_fusion), channel_id=1, source_target_pairs={{0,1},{1,0},{2,3},{3,2},{4,5},{5,4},{6,7},{7,6},{8,9},{9,8},{10,11... | collective-permute-start | bytes 589832 | tf_op jit(solution)/shard_map/ppermute | solution.py:33
  61.2 0.2 collective-permute-start.11
  61.5 2.5 %collective-permute-start.12 = (bf16[256,256]{1,0:T(8,128)(2,1)S(1)}, bf16[256,256]{1,0:T(8,128)(2,1)S(1)}, u32[]{:S(2)}, u32[]{:S(2)}) collective-permute-start(bf16[256,256]{1,0:T(8,128)(2,1)S(1)} %pad_maximum_fusion.4), channel_id=1, source_target_pairs={{0,14},{1,15},{2,0},{3,1},{4,2},{5,3},{6,4},{7,5},{8,6},{9,7},{10,... | collective-permute-start | bytes 393224 | tf_op jit(solution)/shard_map/ppermute | solution.py:33
  64.0 0.8 collective-permute-done.10
  64.9 1.5 %collective-permute-start.13 = (bf16[384,256]{1,0:T(8,128)(2,1)S(1)}, bf16[384,256]{1,0:T(8,128)(2,1)S(1)}, u32[]{:S(2)}, u32[]{:S(2)}) collective-permute-start(bf16[384,256]{1,0:T(8,128)(2,1)S(1)} %collective-permute-done.10), channel_id=1, source_target_pairs={{0,2},{1,3},{2,4},{3,5},{4,6},{5,7},{6,8},{7,9},{8,10},{9,11},{10,... | collective-permute-start | bytes 589832 | tf_op jit(solution)/shard_map/ppermute | solution.py:33
  66.3 0.9 collective-permute-done.11
  67.3 1.0 fusion.8
  68.3 4.3 %collective-permute-done.13 = bf16[384,256]{1,0:T(8,128)(2,1)S(1)} collective-permute-done((bf16[384,256]{1,0:T(8,128)(2,1)S(1)}, bf16[384,256]{1,0:T(8,128)(2,1)S(1)}, u32[]{:S(2)}, u32[]{:S(2)}) %collective-permute-start.13) | collective-permute-done | bytes 196640 | tf_op jit(solution)/shard_map/ppermute | solution.py:33
  72.6 0.6 fusion.20
  73.2 0.2 add_convert_fusion.3
  73.3 4.3 %collective-permute-start.15 = (bf16[1024,256]{1,0:T(8,128)(2,1)S(1)}, bf16[1024,256]{1,0:T(8,128)(2,1)S(1)}, u32[]{:S(2)}, u32[]{:S(2)}) collective-permute-start(bf16[1024,256]{1,0:T(8,128)(2,1)S(1)} %add_convert_fusion.3), channel_id=1, source_target_pairs={{0,16},{16,0},{32,48},{48,32},{64,80},{80,64},{96,112},{112,96},{1... | collective-permute-start | bytes 1572872 | tf_op jit(solution)/shard_map/ppermute | solution.py:37
  77.6 1.0 fusion.2
  78.6 0.6 fusion.14
  79.2 0.2 add_convert_fusion.2
  79.4 12.3 %all_to_all.16 = bf16[8,128,256]{2,1,0:T(8,128)(2,1)S(1)} all-to-all(bf16[8,128,256]{2,1,0:T(8,128)(2,1)S(1)} %bitcast.57), channel_id=1, replica_groups={{0,32,64,96,128,160,192,224},{16,48,80,112,144,176,208,240},{1,33,65,97..., dimensions={0} | all-to-all | bytes 1048576 | tf_op jit(solution)/shard_map/all_to_all | solution.py:139
  91.8 0.1 multiply_reduce_fusion
  92.0 0.1 constant_dynamic-update-slice_fusion.24
  92.1 0.3 collective-permute-start.16
  92.4 1.1 collective-permute-start.17
  93.5 3.7 %collective-permute-done.16 = bf16[128,256]{1,0:T(8,128)(2,1)S(1)} collective-permute-done((bf16[128,256]{1,0:T(8,128)(2,1)S(1)}, bf16[128,256]{1,0:T(8,128)(2,1)S(1)}, u32[]{:S(2)}, u32[]{:S(2)}) %collective-permute-start.16) | collective-permute-done | bytes 65568 | tf_op jit(solution)/shard_map/ppermute | solution.py:33
  97.2 0.4 collective-permute-done.17
  97.6 2.5 %collective-permute-start.18 = (bf16[384,256]{1,0:T(8,128)(2,1)S(1)}, bf16[384,256]{1,0:T(8,128)(2,1)S(1)}, u32[]{:S(2)}, u32[]{:S(2)}) collective-permute-start(bf16[384,256]{1,0:T(8,128)(2,1)S(1)} %pad_maximum_fusion.1), channel_id=1, source_target_pairs={{0,1},{1,0},{2,3},{3,2},{4,5},{5,4},{6,7},{7,6},{8,9},{9,8},{10,11... | collective-permute-start | bytes 589832 | tf_op jit(solution)/shard_map/ppermute | solution.py:33
  100.1 1.8 %collective-permute-start.19 = (bf16[384,256]{1,0:T(8,128)(2,1)S(1)}, bf16[384,256]{1,0:T(8,128)(2,1)S(1)}, u32[]{:S(2)}, u32[]{:S(2)}) collective-permute-start(bf16[384,256]{1,0:T(8,128)(2,1)S(1)} %pad_maximum_fusion.1), channel_id=1, source_target_pairs={{0,2},{1,3},{2,4},{3,5},{4,6},{5,7},{6,8},{7,9},{8,10},{9,11},{10,... | collective-permute-start | bytes 589832 | tf_op jit(solution)/shard_map/ppermute | solution.py:33
  101.9 1.0 collective-permute-start.20
  102.9 0.8 collective-permute-done.18
  103.7 2.0 %collective-permute-start.22 = (bf16[256,256]{1,0:T(8,128)(2,1)S(1)}, bf16[256,256]{1,0:T(8,128)(2,1)S(1)}, u32[]{:S(2)}, u32[]{:S(2)}) collective-permute-start(bf16[256,256]{1,0:T(8,128)(2,1)S(1)} %slice.58), channel_id=1, source_target_pairs={{0,14},{1,15},{2,0},{3,1},{4,2},{5,3},{6,4},{7,5},{8,6},{9,7},{10,... | collective-permute-start | bytes 393224 | tf_op jit(solution)/shard_map/ppermute | solution.py:33
  105.7 0.2 collective-permute-start.21
  106.0 1.0 fusion.6
  107.0 5.9 %collective-permute-done.21 = bf16[384,256]{1,0:T(8,128)(2,1)S(1)} collective-permute-done((bf16[384,256]{1,0:T(8,128)(2,1)S(1)}, bf16[384,256]{1,0:T(8,128)(2,1)S(1)}, u32[]{:S(2)}, u32[]{:S(2)}) %collective-permute-start.21) | collective-permute-done | bytes 196640 | tf_op jit(solution)/shard_map/ppermute | solution.py:33
  112.9 0.6 fusion.18
  113.5 0.2 add_convert_fusion.1
  113.7 4.2 %collective-permute-start.23 = (bf16[1024,256]{1,0:T(8,128)(2,1)S(1)}, bf16[1024,256]{1,0:T(8,128)(2,1)S(1)}, u32[]{:S(2)}, u32[]{:S(2)}) collective-permute-start(bf16[1024,256]{1,0:T(8,128)(2,1)S(1)} %add_convert_fusion.1), channel_id=1, source_target_pairs={{0,16},{16,0},{32,48},{48,32},{64,80},{80,64},{96,112},{112,96},{1... | collective-permute-start | bytes 1572872 | tf_op jit(solution)/shard_map/ppermute | solution.py:37
  117.8 1.0 fusion
  118.8 0.6 fusion.12
  119.4 0.2 add_convert_fusion
  119.6 11.8 %all_to_all.17 = bf16[8,128,256]{2,1,0:T(8,128)(2,1)S(1)} all-to-all(bf16[8,128,256]{2,1,0:T(8,128)(2,1)S(1)} %bitcast.58), channel_id=1, replica_groups={{0,32,64,96,128,160,192,224},{16,48,80,112,144,176,208,240},{1,33,65,97..., dimensions={0} | all-to-all | bytes 1048576 | tf_op jit(solution)/shard_map/all_to_all | solution.py:139
  131.5 0.1 fusion.34
  131.6 0.1 fusion.25
  131.7 0.7 pad_maximum_fusion.2
  (62 shorter events, 1.0 us)
Async XLA Ops:
  0.6 1.0 copy-start
  3.1 14.1 %copy-start.2 = (bf16[128,256]{1,0:T(8,128)(2,1)}, bf16[128,256]{1,0:T(8,128)(2,1)S(1)}, u32[]{:S(2)}) copy-start(bf16[128,256]{1,0:T(8,128)(2,1)S(1)} %multiply_convert_fusion.3.refs_0_) | copy-start | bytes 196612
  3.1 14.1 %collective-permute-start = (bf16[128,256]{1,0:T(8,128)(2,1)S(1)}, bf16[128,256]{1,0:T(8,128)(2,1)S(1)}, u32[]{:S(2)}, u32[]{:S(2)}) collective-permute-start(bf16[128,256]{1,0:T(8,128)(2,1)S(1)} %multiply_convert_fusion.3.refs_0_), channel_id=1, source_target_pairs={{0,10},{1,11},{2,12},{3,13},{4,14},{5,15},{6,0},{7,1},{8,2},{9,3},... | collective-permute-start | bytes 196616 | tf_op jit(solution)/shard_map/ppermute | solution.py:33
  10.5 6.8 %collective-permute-start.1 = (bf16[128,256]{1,0:T(8,128)(2,1)S(1)}, bf16[128,256]{1,0:T(8,128)(2,1)S(1)}, u32[]{:S(2)}, u32[]{:S(2)}) collective-permute-start(bf16[128,256]{1,0:T(8,128)(2,1)S(1)} %multiply_convert_fusion.3.refs_0_), channel_id=1, source_target_pairs={{0,4},{1,5},{2,6},{3,7},{4,8},{5,9},{6,10},{7,11},{8,12},{9,13},{1... | collective-permute-start | bytes 196616 | tf_op jit(solution)/shard_map/ppermute | solution.py:33
  12.4 3.4 %copy-start.1 = (f32[128,128,128]{2,1,0:T(8,128)S(1)}, f32[128,128,128]{2,1,0:T(8,128)}, u32[]{:S(2)}) copy-start(f32[128,128,128]{2,1,0:T(8,128)} %param.9) | copy-start | bytes 25165828
  17.3 7.1 %collective-permute-start.2 = (bf16[384,256]{1,0:T(8,128)(2,1)S(1)}, bf16[384,256]{1,0:T(8,128)(2,1)S(1)}, u32[]{:S(2)}, u32[]{:S(2)}) collective-permute-start(bf16[384,256]{1,0:T(8,128)(2,1)S(1)} %get-tuple-element.13), channel_id=1, source_target_pairs={{0,1},{1,0},{2,3},{3,2},{4,5},{5,4},{6,7},{7,6},{8,9},{9,8},{10,11... | collective-permute-start | bytes 589832 | tf_op jit(solution)/shard_map/ppermute | solution.py:33
  21.5 6.2 %collective-permute-start.3 = (bf16[384,256]{1,0:T(8,128)(2,1)S(1)}, bf16[384,256]{1,0:T(8,128)(2,1)S(1)}, u32[]{:S(2)}, u32[]{:S(2)}) collective-permute-start(bf16[384,256]{1,0:T(8,128)(2,1)S(1)} %get-tuple-element.13), channel_id=1, source_target_pairs={{0,2},{1,3},{2,4},{3,5},{4,6},{5,7},{6,8},{7,9},{8,10},{9,11},{10,... | collective-permute-start | bytes 589832 | tf_op jit(solution)/shard_map/ppermute | solution.py:33
  21.6 6.1 %collective-permute-start.4 = (bf16[256,256]{1,0:T(8,128)(2,1)S(1)}, bf16[256,256]{1,0:T(8,128)(2,1)S(1)}, u32[]{:S(2)}, u32[]{:S(2)}) collective-permute-start(bf16[256,256]{1,0:T(8,128)(2,1)S(1)} %pad_maximum_fusion.3), channel_id=1, source_target_pairs={{0,14},{1,15},{2,0},{3,1},{4,2},{5,3},{6,4},{7,5},{8,6},{9,7},{10,... | collective-permute-start | bytes 393224 | tf_op jit(solution)/shard_map/ppermute | solution.py:33
  24.4 7.5 %collective-permute-start.6 = (bf16[256,256]{1,0:T(8,128)(2,1)S(1)}, bf16[256,256]{1,0:T(8,128)(2,1)S(1)}, u32[]{:S(2)}, u32[]{:S(2)}) collective-permute-start(bf16[256,256]{1,0:T(8,128)(2,1)S(1)} %slice.56), channel_id=1, source_target_pairs={{0,14},{1,15},{2,0},{3,1},{4,2},{5,3},{6,4},{7,5},{8,6},{9,7},{10,... | collective-permute-start | bytes 393224 | tf_op jit(solution)/shard_map/ppermute | solution.py:33
  26.1 5.7 %collective-permute-start.5 = (bf16[384,256]{1,0:T(8,128)(2,1)S(1)}, bf16[384,256]{1,0:T(8,128)(2,1)S(1)}, u32[]{:S(2)}, u32[]{:S(2)}) collective-permute-start(bf16[384,256]{1,0:T(8,128)(2,1)S(1)} %collective-permute-done.2), channel_id=1, source_target_pairs={{0,2},{1,3},{2,4},{3,5},{4,6},{5,7},{6,8},{7,9},{8,10},{9,11},{10,... | collective-permute-start | bytes 589832 | tf_op jit(solution)/shard_map/ppermute | solution.py:33
  32.6 5.3 %collective-permute-start.7 = (bf16[1024,256]{1,0:T(8,128)(2,1)S(1)}, bf16[1024,256]{1,0:T(8,128)(2,1)S(1)}, u32[]{:S(2)}, u32[]{:S(2)}) collective-permute-start(bf16[1024,256]{1,0:T(8,128)(2,1)S(1)} %add_convert_fusion.5), channel_id=1, source_target_pairs={{0,16},{16,0},{32,48},{48,32},{64,80},{80,64},{96,112},{112,96},{1... | collective-permute-start | bytes 1572872 | tf_op jit(solution)/shard_map/ppermute | solution.py:37
  37.3 15.1 %copy-start.3 = (bf16[3,128,256]{2,1,0:T(8,128)(2,1)S(1)}, bf16[3,128,256]{2,1,0:T(8,128)(2,1)}, u32[]{:S(2)}) copy-start(bf16[3,128,256]{2,1,0:T(8,128)(2,1)} %param.11) | copy-start | bytes 589828
  52.6 6.0 %collective-permute-start.8 = (bf16[128,256]{1,0:T(8,128)(2,1)S(1)}, bf16[128,256]{1,0:T(8,128)(2,1)S(1)}, u32[]{:S(2)}, u32[]{:S(2)}) collective-permute-start(bf16[128,256]{1,0:T(8,128)(2,1)S(1)} %get-tuple-element.9), channel_id=1, source_target_pairs={{0,10},{1,11},{2,12},{3,13},{4,14},{5,15},{6,0},{7,1},{8,2},{9,3},... | collective-permute-start | bytes 196616 | tf_op jit(solution)/shard_map/ppermute | solution.py:33
  52.7 5.9 %collective-permute-start.9 = (bf16[128,256]{1,0:T(8,128)(2,1)S(1)}, bf16[128,256]{1,0:T(8,128)(2,1)S(1)}, u32[]{:S(2)}, u32[]{:S(2)}) collective-permute-start(bf16[128,256]{1,0:T(8,128)(2,1)S(1)} %get-tuple-element.9), channel_id=1, source_target_pairs={{0,4},{1,5},{2,6},{3,7},{4,8},{5,9},{6,10},{7,11},{8,12},{9,13},{1... | collective-permute-start | bytes 196616 | tf_op jit(solution)/shard_map/ppermute | solution.py:33
  58.6 6.1 %collective-permute-start.10 = (bf16[384,256]{1,0:T(8,128)(2,1)S(1)}, bf16[384,256]{1,0:T(8,128)(2,1)S(1)}, u32[]{:S(2)}, u32[]{:S(2)}) collective-permute-start(bf16[384,256]{1,0:T(8,128)(2,1)S(1)} %pad_maximum_fusion), channel_id=1, source_target_pairs={{0,1},{1,0},{2,3},{3,2},{4,5},{5,4},{6,7},{7,6},{8,9},{9,8},{10,11... | collective-permute-start | bytes 589832 | tf_op jit(solution)/shard_map/ppermute | solution.py:33
  61.2 6.0 %collective-permute-start.11 = (bf16[384,256]{1,0:T(8,128)(2,1)S(1)}, bf16[384,256]{1,0:T(8,128)(2,1)S(1)}, u32[]{:S(2)}, u32[]{:S(2)}) collective-permute-start(bf16[384,256]{1,0:T(8,128)(2,1)S(1)} %pad_maximum_fusion), channel_id=1, source_target_pairs={{0,2},{1,3},{2,4},{3,5},{4,6},{5,7},{6,8},{7,9},{8,10},{9,11},{10,... | collective-permute-start | bytes 589832 | tf_op jit(solution)/shard_map/ppermute | solution.py:33
  61.5 5.8 %collective-permute-start.12 = (bf16[256,256]{1,0:T(8,128)(2,1)S(1)}, bf16[256,256]{1,0:T(8,128)(2,1)S(1)}, u32[]{:S(2)}, u32[]{:S(2)}) collective-permute-start(bf16[256,256]{1,0:T(8,128)(2,1)S(1)} %pad_maximum_fusion.4), channel_id=1, source_target_pairs={{0,14},{1,15},{2,0},{3,1},{4,2},{5,3},{6,4},{7,5},{8,6},{9,7},{10,... | collective-permute-start | bytes 393224 | tf_op jit(solution)/shard_map/ppermute | solution.py:33
  64.8 7.8 %collective-permute-start.14 = (bf16[256,256]{1,0:T(8,128)(2,1)S(1)}, bf16[256,256]{1,0:T(8,128)(2,1)S(1)}, u32[]{:S(2)}, u32[]{:S(2)}) collective-permute-start(bf16[256,256]{1,0:T(8,128)(2,1)S(1)} %slice.57), channel_id=1, source_target_pairs={{0,14},{1,15},{2,0},{3,1},{4,2},{5,3},{6,4},{7,5},{8,6},{9,7},{10,... | collective-permute-start | bytes 393224 | tf_op jit(solution)/shard_map/ppermute | solution.py:33
  64.9 7.7 %collective-permute-start.13 = (bf16[384,256]{1,0:T(8,128)(2,1)S(1)}, bf16[384,256]{1,0:T(8,128)(2,1)S(1)}, u32[]{:S(2)}, u32[]{:S(2)}) collective-permute-start(bf16[384,256]{1,0:T(8,128)(2,1)S(1)} %collective-permute-done.10), channel_id=1, source_target_pairs={{0,2},{1,3},{2,4},{3,5},{4,6},{5,7},{6,8},{7,9},{8,10},{9,11},{10,... | collective-permute-start | bytes 589832 | tf_op jit(solution)/shard_map/ppermute | solution.py:33
  73.3 5.9 %collective-permute-start.15 = (bf16[1024,256]{1,0:T(8,128)(2,1)S(1)}, bf16[1024,256]{1,0:T(8,128)(2,1)S(1)}, u32[]{:S(2)}, u32[]{:S(2)}) collective-permute-start(bf16[1024,256]{1,0:T(8,128)(2,1)S(1)} %add_convert_fusion.3), channel_id=1, source_target_pairs={{0,16},{16,0},{32,48},{48,32},{64,80},{80,64},{96,112},{112,96},{1... | collective-permute-start | bytes 1572872 | tf_op jit(solution)/shard_map/ppermute | solution.py:37
  92.1 5.1 %collective-permute-start.16 = (bf16[128,256]{1,0:T(8,128)(2,1)S(1)}, bf16[128,256]{1,0:T(8,128)(2,1)S(1)}, u32[]{:S(2)}, u32[]{:S(2)}) collective-permute-start(bf16[128,256]{1,0:T(8,128)(2,1)S(1)} %get-tuple-element.7), channel_id=1, source_target_pairs={{0,10},{1,11},{2,12},{3,13},{4,14},{5,15},{6,0},{7,1},{8,2},{9,3},... | collective-permute-start | bytes 196616 | tf_op jit(solution)/shard_map/ppermute | solution.py:33
  92.4 5.2 %collective-permute-start.17 = (bf16[128,256]{1,0:T(8,128)(2,1)S(1)}, bf16[128,256]{1,0:T(8,128)(2,1)S(1)}, u32[]{:S(2)}, u32[]{:S(2)}) collective-permute-start(bf16[128,256]{1,0:T(8,128)(2,1)S(1)} %get-tuple-element.7), channel_id=1, source_target_pairs={{0,4},{1,5},{2,6},{3,7},{4,8},{5,9},{6,10},{7,11},{8,12},{9,13},{1... | collective-permute-start | bytes 196616 | tf_op jit(solution)/shard_map/ppermute | solution.py:33
  97.6 6.1 %collective-permute-start.18 = (bf16[384,256]{1,0:T(8,128)(2,1)S(1)}, bf16[384,256]{1,0:T(8,128)(2,1)S(1)}, u32[]{:S(2)}, u32[]{:S(2)}) collective-permute-start(bf16[384,256]{1,0:T(8,128)(2,1)S(1)} %pad_maximum_fusion.1), channel_id=1, source_target_pairs={{0,1},{1,0},{2,3},{3,2},{4,5},{5,4},{6,7},{7,6},{8,9},{9,8},{10,11... | collective-permute-start | bytes 589832 | tf_op jit(solution)/shard_map/ppermute | solution.py:33
  100.1 5.8 %collective-permute-start.19 = (bf16[384,256]{1,0:T(8,128)(2,1)S(1)}, bf16[384,256]{1,0:T(8,128)(2,1)S(1)}, u32[]{:S(2)}, u32[]{:S(2)}) collective-permute-start(bf16[384,256]{1,0:T(8,128)(2,1)S(1)} %pad_maximum_fusion.1), channel_id=1, source_target_pairs={{0,2},{1,3},{2,4},{3,5},{4,6},{5,7},{6,8},{7,9},{8,10},{9,11},{10,... | collective-permute-start | bytes 589832 | tf_op jit(solution)/shard_map/ppermute | solution.py:33
  101.9 4.0 %collective-permute-start.20 = (bf16[256,256]{1,0:T(8,128)(2,1)S(1)}, bf16[256,256]{1,0:T(8,128)(2,1)S(1)}, u32[]{:S(2)}, u32[]{:S(2)}) collective-permute-start(bf16[256,256]{1,0:T(8,128)(2,1)S(1)} %pad_maximum_fusion.5), channel_id=1, source_target_pairs={{0,14},{1,15},{2,0},{3,1},{4,2},{5,3},{6,4},{7,5},{8,6},{9,7},{10,... | collective-permute-start | bytes 393224 | tf_op jit(solution)/shard_map/ppermute | solution.py:33
  103.7 9.1 %collective-permute-start.22 = (bf16[256,256]{1,0:T(8,128)(2,1)S(1)}, bf16[256,256]{1,0:T(8,128)(2,1)S(1)}, u32[]{:S(2)}, u32[]{:S(2)}) collective-permute-start(bf16[256,256]{1,0:T(8,128)(2,1)S(1)} %slice.58), channel_id=1, source_target_pairs={{0,14},{1,15},{2,0},{3,1},{4,2},{5,3},{6,4},{7,5},{8,6},{9,7},{10,... | collective-permute-start | bytes 393224 | tf_op jit(solution)/shard_map/ppermute | solution.py:33
  105.7 7.1 %collective-permute-start.21 = (bf16[384,256]{1,0:T(8,128)(2,1)S(1)}, bf16[384,256]{1,0:T(8,128)(2,1)S(1)}, u32[]{:S(2)}, u32[]{:S(2)}) collective-permute-start(bf16[384,256]{1,0:T(8,128)(2,1)S(1)} %collective-permute-done.18), channel_id=1, source_target_pairs={{0,2},{1,3},{2,4},{3,5},{4,6},{5,7},{6,8},{7,9},{8,10},{9,11},{10,... | collective-permute-start | bytes 589832 | tf_op jit(solution)/shard_map/ppermute | solution.py:33
  113.7 5.8 %collective-permute-start.23 = (bf16[1024,256]{1,0:T(8,128)(2,1)S(1)}, bf16[1024,256]{1,0:T(8,128)(2,1)S(1)}, u32[]{:S(2)}, u32[]{:S(2)}) collective-permute-start(bf16[1024,256]{1,0:T(8,128)(2,1)S(1)} %add_convert_fusion.1), channel_id=1, source_target_pairs={{0,16},{16,0},{32,48},{48,32},{64,80},{80,64},{96,112},{112,96},{1... | collective-permute-start | bytes 1572872 | tf_op jit(solution)/shard_map/ppermute | solution.py:37
where the time goes:
time: 133 us; the launch traced here: 132 us
  starting transfers between devices  45.5 us (34%)
  blocking collectives  38.3 us (29%)
  waiting for transfers between devices  25.7 us (19%)
  matrix products  10.8 us (8%)
  local copies, waits for them, and re-layouts  4.62 us (3%)
  other arithmetic  3.61 us (3%)
  Pallas kernels  2.78 us (2%)
    all_to_all x3, blocking collectives, shards(): lax.all_to_all(mine.astype(BF).reshape(NY * NX, BS, -1), 'src', 0, 0, axi...  38.3 us
    ppermute x21, starting transfers between devices, shift_dst(): return lax.ppermute(x, 'dst', perm)  33.4 us
    ppermute x21, waiting for transfers between devices, shift_dst(): return lax.ppermute(x, 'dst', perm)  25.7 us
    ppermute x3, starting transfers between devices, swap_core(): return lax.ppermute(x, 'src', [(i, i ^ 1) for i in range(NY * NX * 2)])  12.1 us
    dot_general x6, matrix products, early(): jnp.dot(a[:, :n], near, preferred_element_type=F32)  5.91 us
    unnamed x23, local copies, waits for them, and re-layouts  4.51 us
    dot_general x6, matrix products, late(): return jnp.dot(a[:, n:], rest, preferred_element_type=F32)  3.47 us
    pallas_call x2, Pallas kernels, pack(): pl.pallas_call(functools.partial(pack_kernel, other), out_shape=[jax.Shap...  2.78 us
  transfers between devices with their start and end apart: 24, of which 10 were waited for; matrix products, arithmetic and copies ran while one was open for 7% of the time, Pallas kernels for 2%

commit v1 on v0

--- a/solution.py
+++ b/solution.py
@@ -29,8 +29,13 @@
 
 
 def shift_dst(x, dz, flip=0):
-    perm = [(i, ((i // 2 + dz) % NZ) * 2 + ((i % 2) ^ flip)) for i in range(NZ * 2)]
-    return lax.ppermute(x, "dst", perm)
+    perm = []
+    for s in range(NY * NX * 2):
+        step = -dz if s % 2 else dz
+        for d in range(NZ * 2):
+            to = ((d // 2 + step) % NZ) * 2 + ((d % 2) ^ flip)
+            perm.append((s * NZ * 2 + d, s * NZ * 2 + to))
+    return lax.ppermute(x, ("src", "dst"), perm)
 
 
 def swap_core(x):
@@ -69,7 +74,7 @@
         table = jnp.where(
             (col & 1) == xh, jnp.int32(as_int32(SLOTS[0])), jnp.int32(as_int32(SLOTS[1]))
         )
-        shift = (((col >> 1) - z) & (NZ - 1)) * 4
+        shift = (((col >> 1) - z) * (1 - 2 * core) & (NZ - 1)) * 4
         at = pl.multiple_of(((table >> shift) & 15) * BS, BS)
         o_ref[pl.ds(row, BS), pl.ds(at, BS)] = w_ref[0, 0, j].astype(BF)
 

time: 133 us -> 134 us (level)
  starting transfers between devices: 45.5 us -> 50.3 us
  waiting for transfers between devices: 25.7 us -> 22.4 us
    ppermute x21, starting transfers between devices: 33.4 us -> 39.2 us  [shift_dst(): return lax.ppermute(x, ('src', 'dst'), perm)]
    ppermute x21, waiting for transfers between devices: 25.7 us -> 22.4 us  [shift_dst(): return lax.ppermute(x, ('src', 'dst'), perm)]
  transfers between devices with their start and end apart: 24 -> 24, of which waited for: 10 -> 10; matrix products, arithmetic and copies ran while one was open for 7% -> 6% of each run, Pallas kernels for 2% -> 2%
where the time goes in v1:
time: 134 us
  starting transfers between devices  50.3 us (38%)
  blocking collectives  38.4 us (29%)
  waiting for transfers between devices  22.4 us (17%)
  matrix products  10.8 us (8%)
  local copies, waits for them, and re-layouts  4.62 us (3%)
  other arithmetic  3.61 us (3%)
  Pallas kernels  2.84 us (2%)
    ppermute x21, starting transfers between devices, shift_dst(): return lax.ppermute(x, ('src', 'dst'), perm)  39.2 us
    all_to_all x3, blocking collectives, shards(): lax.all_to_all(mine.astype(BF).reshape(NY * NX, BS, -1), 'src', 0, 0, axi...  38.4 us
    ppermute x21, waiting for transfers between devices, shift_dst(): return lax.ppermute(x, ('src', 'dst'), perm)  22.4 us
    ppermute x3, starting transfers between devices, swap_core(): return lax.ppermute(x, 'src', [(i, i ^ 1) for i in range(NY * NX * 2)])  11 us
    dot_general x6, matrix products, early(): jnp.dot(a[:, :n], near, preferred_element_type=F32)  5.92 us
    unnamed x23, local copies, waits for them, and re-layouts  4.51 us
    dot_general x6, matrix products, late(): return jnp.dot(a[:, n:], rest, preferred_element_type=F32)  3.47 us
    pallas_call x2, Pallas kernels, pack(): pl.pallas_call(functools.partial(pack_kernel, other), out_shape=[jax.Shap...  2.84 us
  transfers between devices with their start and end apart: 24, of which 10 were waited for; matrix products, arithmetic and copies ran while one was open for 6% of the time, Pallas kernels for 2%

profile of v1, /device:TPU:1, one launch (start us, length us, event | category | flops | bytes accessed | tf_op | source)
XLA Modules:
  0.0 134.1 jit_solution(16158070139173347090)
XLA Ops:
  0.6 0.9 copy-done
  1.6 1.4 %multiply_reduce_fusion.2 = (f32[128]{0:T(128)S(1)}, f32[128,256]{1,0:T(8,128)S(1)}) fusion(bf16[512,256]{1,0:T(8,128)(2,1)S(1)} %copy-done, bf16[128,256]{1,0:T(8,128)(2,1)} %param.6, bf16[256,512]{1,0:T(8,128)(2,1)} %param.7), kind=kOutput, calls=%fused_computation.62 | convolution fusion | flops 67501952 | bytes 721408 | tf_op jit(solution)/shard_map/dot_general | solution.py:120
  3.1 5.3 %collective-permute-start = (bf16[128,256]{1,0:T(8,128)(2,1)S(1)}, bf16[128,256]{1,0:T(8,128)(2,1)S(1)}, u32[]{:S(2)}, u32[]{:S(2)}) collective-permute-start(bf16[128,256]{1,0:T(8,128)(2,1)S(1)} %multiply_convert_fusion.3.refs_0_), channel_id=1, source_target_pairs={{0,10},{1,11},{2,12},{3,13},{4,14},{5,15},{6,0},{7,1},{8,2},{9,3},... | collective-permute-start | bytes 196616 | tf_op jit(solution)/shard_map/ppermute | solution.py:38
  8.4 1.8 %collective-permute-start.1 = (bf16[128,256]{1,0:T(8,128)(2,1)S(1)}, bf16[128,256]{1,0:T(8,128)(2,1)S(1)}, u32[]{:S(2)}, u32[]{:S(2)}) collective-permute-start(bf16[128,256]{1,0:T(8,128)(2,1)S(1)} %multiply_convert_fusion.3.refs_0_), channel_id=1, source_target_pairs={{0,4},{1,5},{2,6},{3,7},{4,8},{5,9},{6,10},{7,11},{8,12},{9,13},{1... | collective-permute-start | bytes 196616 | tf_op jit(solution)/shard_map/ppermute | solution.py:38
  10.1 0.7 pad_add_fusion.info_ref
  10.9 3.4 %copy-done.1 = f32[128,128,128]{2,1,0:T(8,128)S(1)} copy-done((f32[128,128,128]{2,1,0:T(8,128)S(1)}, f32[128,128,128]{2,1,0:T(8,128)}, u32[]{:S(2)}) %copy-start.1) | copy-done | bytes 8388632
  14.3 1.4 %pack.3 = (bf16[1024,2048]{1,0:T(8,128)(2,1)S(1)}, bf16[128,256]{1,0:T(8,128)(2,1)S(1)}) custom-call(s32[131]{0:T(256)S(1)} %pad_add_fusion.info_ref, f32[8,2,8,128,128]{4,3,2,1,0:T(8,128)S(1)} %bitcast.54, bf16[128,256]{1,0:T(8,128)(2,1)S(1)} %multiply_convert_fusion.3.refs_0_), custom_call_target="tpu_custom_call" | custom-call | bytes 6291456 | tf_op jit(solution)/shard_map/pack/pallas_call | solution.py:86
  15.8 2.8 %collective-permute-start.2 = (bf16[384,256]{1,0:T(8,128)(2,1)S(1)}, bf16[384,256]{1,0:T(8,128)(2,1)S(1)}, u32[]{:S(2)}, u32[]{:S(2)}) collective-permute-start(bf16[384,256]{1,0:T(8,128)(2,1)S(1)} %get-tuple-element.13), channel_id=1, source_target_pairs={{0,1},{1,0},{2,3},{3,2},{4,5},{5,4},{6,7},{7,6},{8,9},{9,8},{10,11... | collective-permute-start | bytes 589832 | tf_op jit(solution)/shard_map/ppermute | solution.py:38
  18.6 1.4 %pack.2 = bf16[1024,2048]{1,0:T(8,128)(2,1)S(1)} custom-call(s32[131]{0:T(256)S(1)} %pad_add_fusion.info_ref, f32[8,2,8,128,128]{4,3,2,1,0:T(8,128)S(1)} %bitcast.55), custom_call_target="tpu_custom_call" | custom-call | bytes 6291456 | tf_op jit(solution)/shard_map/pack/pallas_call | solution.py:86
  20.0 0.8 collective-permute-start.3
  20.9 0.8 collective-permute-start.4
  21.7 0.2 collective-permute-done.2
  21.9 1.2 collective-permute-start.6
  23.1 1.6 %collective-permute-start.5 = (bf16[384,256]{1,0:T(8,128)(2,1)S(1)}, bf16[384,256]{1,0:T(8,128)(2,1)S(1)}, u32[]{:S(2)}, u32[]{:S(2)}) collective-permute-start(bf16[384,256]{1,0:T(8,128)(2,1)S(1)} %collective-permute-done.2), channel_id=1, source_target_pairs={{0,2},{1,3},{2,4},{3,5},{4,6},{5,7},{6,8},{7,9},{8,10},{9,11},{10,... | collective-permute-start | bytes 589832 | tf_op jit(solution)/shard_map/ppermute | solution.py:38
  24.7 0.3 collective-permute-done.3
  25.0 1.0 collective-permute-done.4
  26.0 1.0 fusion.10
  27.0 1.6 %collective-permute-done.5 = bf16[384,256]{1,0:T(8,128)(2,1)S(1)} collective-permute-done((bf16[384,256]{1,0:T(8,128)(2,1)S(1)}, bf16[384,256]{1,0:T(8,128)(2,1)S(1)}, u32[]{:S(2)}, u32[]{:S(2)}) %collective-permute-start.5) | collective-permute-done | bytes 196640 | tf_op jit(solution)/shard_map/ppermute | solution.py:38
  28.7 0.6 fusion.22
  29.2 0.2 add_convert_fusion.5
  29.4 6.5 %collective-permute-start.7 = (bf16[1024,256]{1,0:T(8,128)(2,1)S(1)}, bf16[1024,256]{1,0:T(8,128)(2,1)S(1)}, u32[]{:S(2)}, u32[]{:S(2)}) collective-permute-start(bf16[1024,256]{1,0:T(8,128)(2,1)S(1)} %add_convert_fusion.5), channel_id=1, source_target_pairs={{0,16},{16,0},{32,48},{48,32},{64,80},{80,64},{96,112},{112,96},{1... | collective-permute-start | bytes 1572872 | tf_op jit(solution)/shard_map/ppermute | solution.py:42
  35.9 1.0 fusion.4
  36.9 0.6 fusion.16
  37.5 0.2 add_convert_fusion.4
  37.7 14.2 %all_to_all.15 = bf16[8,128,256]{2,1,0:T(8,128)(2,1)S(1)} all-to-all(bf16[8,128,256]{2,1,0:T(8,128)(2,1)S(1)} %bitcast.56), channel_id=1, replica_groups={{0,32,64,96,128,160,192,224},{16,48,80,112,144,176,208,240},{1,33,65,97..., dimensions={0} | all-to-all | bytes 1048576 | tf_op jit(solution)/shard_map/all_to_all | solution.py:144
  52.0 0.1 multiply_reduce_fusion.1
  52.2 0.8 collective-permute-start.8
  53.0 1.1 collective-permute-start.9
  54.1 5.0 %collective-permute-done.8 = bf16[128,256]{1,0:T(8,128)(2,1)S(1)} collective-permute-done((bf16[128,256]{1,0:T(8,128)(2,1)S(1)}, bf16[128,256]{1,0:T(8,128)(2,1)S(1)}, u32[]{:S(2)}, u32[]{:S(2)}) %collective-permute-start.8) | collective-permute-done | bytes 65568 | tf_op jit(solution)/shard_map/ppermute | solution.py:38
  59.2 2.5 %collective-permute-start.10 = (bf16[384,256]{1,0:T(8,128)(2,1)S(1)}, bf16[384,256]{1,0:T(8,128)(2,1)S(1)}, u32[]{:S(2)}, u32[]{:S(2)}) collective-permute-start(bf16[384,256]{1,0:T(8,128)(2,1)S(1)} %pad_maximum_fusion), channel_id=1, source_target_pairs={{0,1},{1,0},{2,3},{3,2},{4,5},{5,4},{6,7},{7,6},{8,9},{9,8},{10,11... | collective-permute-start | bytes 589832 | tf_op jit(solution)/shard_map/ppermute | solution.py:38
  61.7 1.3 collective-permute-start.11
  63.0 1.4 %collective-permute-start.12 = (bf16[256,256]{1,0:T(8,128)(2,1)S(1)}, bf16[256,256]{1,0:T(8,128)(2,1)S(1)}, u32[]{:S(2)}, u32[]{:S(2)}) collective-permute-start(bf16[256,256]{1,0:T(8,128)(2,1)S(1)} %pad_maximum_fusion.4), channel_id=1, source_target_pairs={{0,14},{1,15},{2,0},{3,1},{4,2},{5,3},{6,4},{7,5},{8,6},{9,7},{10,... | collective-permute-start | bytes 393224 | tf_op jit(solution)/shard_map/ppermute | solution.py:38
  64.5 0.8 collective-permute-done.10
  65.3 3.8 %collective-permute-start.14 = (bf16[256,256]{1,0:T(8,128)(2,1)S(1)}, bf16[256,256]{1,0:T(8,128)(2,1)S(1)}, u32[]{:S(2)}, u32[]{:S(2)}) collective-permute-start(bf16[256,256]{1,0:T(8,128)(2,1)S(1)} %slice.57), channel_id=1, source_target_pairs={{0,14},{1,15},{2,0},{3,1},{4,2},{5,3},{6,4},{7,5},{8,6},{9,7},{10,... | collective-permute-start | bytes 393224 | tf_op jit(solution)/shard_map/ppermute | solution.py:38
  69.1 1.0 fusion.8
  70.1 5.1 %collective-permute-done.13 = bf16[384,256]{1,0:T(8,128)(2,1)S(1)} collective-permute-done((bf16[384,256]{1,0:T(8,128)(2,1)S(1)}, bf16[384,256]{1,0:T(8,128)(2,1)S(1)}, u32[]{:S(2)}, u32[]{:S(2)}) %collective-permute-start.13) | collective-permute-done | bytes 196640 | tf_op jit(solution)/shard_map/ppermute | solution.py:38
  75.3 0.6 fusion.20
  75.9 0.2 add_convert_fusion.3
  76.0 1.8 %collective-permute-start.15 = (bf16[1024,256]{1,0:T(8,128)(2,1)S(1)}, bf16[1024,256]{1,0:T(8,128)(2,1)S(1)}, u32[]{:S(2)}, u32[]{:S(2)}) collective-permute-start(bf16[1024,256]{1,0:T(8,128)(2,1)S(1)} %add_convert_fusion.3), channel_id=1, source_target_pairs={{0,16},{16,0},{32,48},{48,32},{64,80},{80,64},{96,112},{112,96},{1... | collective-permute-start | bytes 1572872 | tf_op jit(solution)/shard_map/ppermute | solution.py:42
  77.8 1.0 fusion.2
  78.8 0.6 fusion.14
  79.4 0.2 add_convert_fusion.2
  79.6 12.1 %all_to_all.16 = bf16[8,128,256]{2,1,0:T(8,128)(2,1)S(1)} all-to-all(bf16[8,128,256]{2,1,0:T(8,128)(2,1)S(1)} %bitcast.57), channel_id=1, replica_groups={{0,32,64,96,128,160,192,224},{16,48,80,112,144,176,208,240},{1,33,65,97..., dimensions={0} | all-to-all | bytes 1048576 | tf_op jit(solution)/shard_map/all_to_all | solution.py:144
  91.8 0.1 multiply_reduce_fusion
  92.1 0.4 collective-permute-start.16
  92.4 2.6 %collective-permute-start.17 = (bf16[128,256]{1,0:T(8,128)(2,1)S(1)}, bf16[128,256]{1,0:T(8,128)(2,1)S(1)}, u32[]{:S(2)}, u32[]{:S(2)}) collective-permute-start(bf16[128,256]{1,0:T(8,128)(2,1)S(1)} %get-tuple-element.7), channel_id=1, source_target_pairs={{0,4},{1,5},{2,6},{3,7},{4,8},{5,9},{6,10},{7,11},{8,12},{9,13},{1... | collective-permute-start | bytes 196616 | tf_op jit(solution)/shard_map/ppermute | solution.py:38
  95.1 3.4 %collective-permute-done.16 = bf16[128,256]{1,0:T(8,128)(2,1)S(1)} collective-permute-done((bf16[128,256]{1,0:T(8,128)(2,1)S(1)}, bf16[128,256]{1,0:T(8,128)(2,1)S(1)}, u32[]{:S(2)}, u32[]{:S(2)}) %collective-permute-start.16) | collective-permute-done | bytes 65568 | tf_op jit(solution)/shard_map/ppermute | solution.py:38
  98.5 2.5 %collective-permute-start.18 = (bf16[384,256]{1,0:T(8,128)(2,1)S(1)}, bf16[384,256]{1,0:T(8,128)(2,1)S(1)}, u32[]{:S(2)}, u32[]{:S(2)}) collective-permute-start(bf16[384,256]{1,0:T(8,128)(2,1)S(1)} %pad_maximum_fusion.1), channel_id=1, source_target_pairs={{0,1},{1,0},{2,3},{3,2},{4,5},{5,4},{6,7},{7,6},{8,9},{9,8},{10,11... | collective-permute-start | bytes 589832 | tf_op jit(solution)/shard_map/ppermute | solution.py:38
  101.0 3.6 %collective-permute-start.19 = (bf16[384,256]{1,0:T(8,128)(2,1)S(1)}, bf16[384,256]{1,0:T(8,128)(2,1)S(1)}, u32[]{:S(2)}, u32[]{:S(2)}) collective-permute-start(bf16[384,256]{1,0:T(8,128)(2,1)S(1)} %pad_maximum_fusion.1), channel_id=1, source_target_pairs={{0,2},{1,3},{2,4},{3,5},{4,6},{5,7},{6,8},{7,9},{8,10},{9,11},{10,... | collective-permute-start | bytes 589832 | tf_op jit(solution)/shard_map/ppermute | solution.py:38
  104.6 0.4 collective-permute-start.20
  105.1 4.5 %collective-permute-start.22 = (bf16[256,256]{1,0:T(8,128)(2,1)S(1)}, bf16[256,256]{1,0:T(8,128)(2,1)S(1)}, u32[]{:S(2)}, u32[]{:S(2)}) collective-permute-start(bf16[256,256]{1,0:T(8,128)(2,1)S(1)} %slice.58), channel_id=1, source_target_pairs={{0,14},{1,15},{2,0},{3,1},{4,2},{5,3},{6,4},{7,5},{8,6},{9,7},{10,... | collective-permute-start | bytes 393224 | tf_op jit(solution)/shard_map/ppermute | solution.py:38
  109.5 0.1 collective-permute-start.21
  109.7 0.9 collective-permute-done.20
  110.6 1.0 fusion.6
  111.5 4.0 %collective-permute-done.21 = bf16[384,256]{1,0:T(8,128)(2,1)S(1)} collective-permute-done((bf16[384,256]{1,0:T(8,128)(2,1)S(1)}, bf16[384,256]{1,0:T(8,128)(2,1)S(1)}, u32[]{:S(2)}, u32[]{:S(2)}) %collective-permute-start.21) | collective-permute-done | bytes 196640 | tf_op jit(solution)/shard_map/ppermute | solution.py:38
  115.6 0.6 fusion.18
  116.2 0.2 add_convert_fusion.1
  116.4 2.7 %collective-permute-start.23 = (bf16[1024,256]{1,0:T(8,128)(2,1)S(1)}, bf16[1024,256]{1,0:T(8,128)(2,1)S(1)}, u32[]{:S(2)}, u32[]{:S(2)}) collective-permute-start(bf16[1024,256]{1,0:T(8,128)(2,1)S(1)} %add_convert_fusion.1), channel_id=1, source_target_pairs={{0,16},{16,0},{32,48},{48,32},{64,80},{80,64},{96,112},{112,96},{1... | collective-permute-start | bytes 1572872 | tf_op jit(solution)/shard_map/ppermute | solution.py:42
  119.1 1.0 fusion
  120.1 0.6 fusion.12
  120.7 0.2 add_convert_fusion
  120.9 12.1 %all_to_all.17 = bf16[8,128,256]{2,1,0:T(8,128)(2,1)S(1)} all-to-all(bf16[8,128,256]{2,1,0:T(8,128)(2,1)S(1)} %bitcast.58), channel_id=1, replica_groups={{0,32,64,96,128,160,192,224},{16,48,80,112,144,176,208,240},{1,33,65,97..., dimensions={0} | all-to-all | bytes 1048576 | tf_op jit(solution)/shard_map/all_to_all | solution.py:144
  133.3 0.1 fusion.25
  133.4 0.7 pad_maximum_fusion.2
  (62 shorter events, 1.0 us)
Async XLA Ops:
  0.6 1.0 copy-start
  3.1 12.6 %copy-start.2 = (bf16[128,256]{1,0:T(8,128)(2,1)}, bf16[128,256]{1,0:T(8,128)(2,1)S(1)}, u32[]{:S(2)}) copy-start(bf16[128,256]{1,0:T(8,128)(2,1)S(1)} %multiply_convert_fusion.3.refs_0_) | copy-start | bytes 196612
  3.1 12.6 %collective-permute-start = (bf16[128,256]{1,0:T(8,128)(2,1)S(1)}, bf16[128,256]{1,0:T(8,128)(2,1)S(1)}, u32[]{:S(2)}, u32[]{:S(2)}) collective-permute-start(bf16[128,256]{1,0:T(8,128)(2,1)S(1)} %multiply_convert_fusion.3.refs_0_), channel_id=1, source_target_pairs={{0,10},{1,11},{2,12},{3,13},{4,14},{5,15},{6,0},{7,1},{8,2},{9,3},... | collective-permute-start | bytes 196616 | tf_op jit(solution)/shard_map/ppermute | solution.py:38
  8.4 7.4 %collective-permute-start.1 = (bf16[128,256]{1,0:T(8,128)(2,1)S(1)}, bf16[128,256]{1,0:T(8,128)(2,1)S(1)}, u32[]{:S(2)}, u32[]{:S(2)}) collective-permute-start(bf16[128,256]{1,0:T(8,128)(2,1)S(1)} %multiply_convert_fusion.3.refs_0_), channel_id=1, source_target_pairs={{0,4},{1,5},{2,6},{3,7},{4,8},{5,9},{6,10},{7,11},{8,12},{9,13},{1... | collective-permute-start | bytes 196616 | tf_op jit(solution)/shard_map/ppermute | solution.py:38
  10.9 3.4 %copy-start.1 = (f32[128,128,128]{2,1,0:T(8,128)S(1)}, f32[128,128,128]{2,1,0:T(8,128)}, u32[]{:S(2)}) copy-start(f32[128,128,128]{2,1,0:T(8,128)} %param.9) | copy-start | bytes 25165828
  15.8 6.1 %collective-permute-start.2 = (bf16[384,256]{1,0:T(8,128)(2,1)S(1)}, bf16[384,256]{1,0:T(8,128)(2,1)S(1)}, u32[]{:S(2)}, u32[]{:S(2)}) collective-permute-start(bf16[384,256]{1,0:T(8,128)(2,1)S(1)} %get-tuple-element.13), channel_id=1, source_target_pairs={{0,1},{1,0},{2,3},{3,2},{4,5},{5,4},{6,7},{7,6},{8,9},{9,8},{10,11... | collective-permute-start | bytes 589832 | tf_op jit(solution)/shard_map/ppermute | solution.py:38
  20.0 4.9 %collective-permute-start.3 = (bf16[384,256]{1,0:T(8,128)(2,1)S(1)}, bf16[384,256]{1,0:T(8,128)(2,1)S(1)}, u32[]{:S(2)}, u32[]{:S(2)}) collective-permute-start(bf16[384,256]{1,0:T(8,128)(2,1)S(1)} %get-tuple-element.13), channel_id=1, source_target_pairs={{0,2},{1,3},{2,4},{3,5},{4,6},{5,7},{6,8},{7,9},{8,10},{9,11},{10,... | collective-permute-start | bytes 589832 | tf_op jit(solution)/shard_map/ppermute | solution.py:38
  20.9 5.1 %collective-permute-start.4 = (bf16[256,256]{1,0:T(8,128)(2,1)S(1)}, bf16[256,256]{1,0:T(8,128)(2,1)S(1)}, u32[]{:S(2)}, u32[]{:S(2)}) collective-permute-start(bf16[256,256]{1,0:T(8,128)(2,1)S(1)} %pad_maximum_fusion.3), channel_id=1, source_target_pairs={{0,14},{1,15},{2,0},{3,1},{4,2},{5,3},{6,4},{7,5},{8,6},{9,7},{10,... | collective-permute-start | bytes 393224 | tf_op jit(solution)/shard_map/ppermute | solution.py:38
  21.9 6.7 %collective-permute-start.6 = (bf16[256,256]{1,0:T(8,128)(2,1)S(1)}, bf16[256,256]{1,0:T(8,128)(2,1)S(1)}, u32[]{:S(2)}, u32[]{:S(2)}) collective-permute-start(bf16[256,256]{1,0:T(8,128)(2,1)S(1)} %slice.56), channel_id=1, source_target_pairs={{0,14},{1,15},{2,0},{3,1},{4,2},{5,3},{6,4},{7,5},{8,6},{9,7},{10,... | collective-permute-start | bytes 393224 | tf_op jit(solution)/shard_map/ppermute | solution.py:38
  23.1 5.6 %collective-permute-start.5 = (bf16[384,256]{1,0:T(8,128)(2,1)S(1)}, bf16[384,256]{1,0:T(8,128)(2,1)S(1)}, u32[]{:S(2)}, u32[]{:S(2)}) collective-permute-start(bf16[384,256]{1,0:T(8,128)(2,1)S(1)} %collective-permute-done.2), channel_id=1, source_target_pairs={{0,2},{1,3},{2,4},{3,5},{4,6},{5,7},{6,8},{7,9},{8,10},{9,11},{10,... | collective-permute-start | bytes 589832 | tf_op jit(solution)/shard_map/ppermute | solution.py:38
  29.4 8.1 %collective-permute-start.7 = (bf16[1024,256]{1,0:T(8,128)(2,1)S(1)}, bf16[1024,256]{1,0:T(8,128)(2,1)S(1)}, u32[]{:S(2)}, u32[]{:S(2)}) collective-permute-start(bf16[1024,256]{1,0:T(8,128)(2,1)S(1)} %add_convert_fusion.5), channel_id=1, source_target_pairs={{0,16},{16,0},{32,48},{48,32},{64,80},{80,64},{96,112},{112,96},{1... | collective-permute-start | bytes 1572872 | tf_op jit(solution)/shard_map/ppermute | solution.py:42
  36.9 15.1 %copy-start.3 = (bf16[3,128,256]{2,1,0:T(8,128)(2,1)S(1)}, bf16[3,128,256]{2,1,0:T(8,128)(2,1)}, u32[]{:S(2)}) copy-start(bf16[3,128,256]{2,1,0:T(8,128)(2,1)} %param.11) | copy-start | bytes 589828
  52.2 6.9 %collective-permute-start.8 = (bf16[128,256]{1,0:T(8,128)(2,1)S(1)}, bf16[128,256]{1,0:T(8,128)(2,1)S(1)}, u32[]{:S(2)}, u32[]{:S(2)}) collective-permute-start(bf16[128,256]{1,0:T(8,128)(2,1)S(1)} %get-tuple-element.9), channel_id=1, source_target_pairs={{0,10},{1,11},{2,12},{3,13},{4,14},{5,15},{6,0},{7,1},{8,2},{9,3},... | collective-permute-start | bytes 196616 | tf_op jit(solution)/shard_map/ppermute | solution.py:38
  53.0 6.1 %collective-permute-start.9 = (bf16[128,256]{1,0:T(8,128)(2,1)S(1)}, bf16[128,256]{1,0:T(8,128)(2,1)S(1)}, u32[]{:S(2)}, u32[]{:S(2)}) collective-permute-start(bf16[128,256]{1,0:T(8,128)(2,1)S(1)} %get-tuple-element.9), channel_id=1, source_target_pairs={{0,4},{1,5},{2,6},{3,7},{4,8},{5,9},{6,10},{7,11},{8,12},{9,13},{1... | collective-permute-start | bytes 196616 | tf_op jit(solution)/shard_map/ppermute | solution.py:38
  59.2 6.1 %collective-permute-start.10 = (bf16[384,256]{1,0:T(8,128)(2,1)S(1)}, bf16[384,256]{1,0:T(8,128)(2,1)S(1)}, u32[]{:S(2)}, u32[]{:S(2)}) collective-permute-start(bf16[384,256]{1,0:T(8,128)(2,1)S(1)} %pad_maximum_fusion), channel_id=1, source_target_pairs={{0,1},{1,0},{2,3},{3,2},{4,5},{5,4},{6,7},{7,6},{8,9},{9,8},{10,11... | collective-permute-start | bytes 589832 | tf_op jit(solution)/shard_map/ppermute | solution.py:38
  61.7 7.4 %collective-permute-start.11 = (bf16[384,256]{1,0:T(8,128)(2,1)S(1)}, bf16[384,256]{1,0:T(8,128)(2,1)S(1)}, u32[]{:S(2)}, u32[]{:S(2)}) collective-permute-start(bf16[384,256]{1,0:T(8,128)(2,1)S(1)} %pad_maximum_fusion), channel_id=1, source_target_pairs={{0,2},{1,3},{2,4},{3,5},{4,6},{5,7},{6,8},{7,9},{8,10},{9,11},{10,... | collective-permute-start | bytes 589832 | tf_op jit(solution)/shard_map/ppermute | solution.py:38
  63.0 6.1 %collective-permute-start.12 = (bf16[256,256]{1,0:T(8,128)(2,1)S(1)}, bf16[256,256]{1,0:T(8,128)(2,1)S(1)}, u32[]{:S(2)}, u32[]{:S(2)}) collective-permute-start(bf16[256,256]{1,0:T(8,128)(2,1)S(1)} %pad_maximum_fusion.4), channel_id=1, source_target_pairs={{0,14},{1,15},{2,0},{3,1},{4,2},{5,3},{6,4},{7,5},{8,6},{9,7},{10,... | collective-permute-start | bytes 393224 | tf_op jit(solution)/shard_map/ppermute | solution.py:38
  65.3 10.0 %collective-permute-start.14 = (bf16[256,256]{1,0:T(8,128)(2,1)S(1)}, bf16[256,256]{1,0:T(8,128)(2,1)S(1)}, u32[]{:S(2)}, u32[]{:S(2)}) collective-permute-start(bf16[256,256]{1,0:T(8,128)(2,1)S(1)} %slice.57), channel_id=1, source_target_pairs={{0,14},{1,15},{2,0},{3,1},{4,2},{5,3},{6,4},{7,5},{8,6},{9,7},{10,... | collective-permute-start | bytes 393224 | tf_op jit(solution)/shard_map/ppermute | solution.py:38
  69.1 6.2 %collective-permute-start.13 = (bf16[384,256]{1,0:T(8,128)(2,1)S(1)}, bf16[384,256]{1,0:T(8,128)(2,1)S(1)}, u32[]{:S(2)}, u32[]{:S(2)}) collective-permute-start(bf16[384,256]{1,0:T(8,128)(2,1)S(1)} %collective-permute-done.10), channel_id=1, source_target_pairs={{0,2},{1,3},{2,4},{3,5},{4,6},{5,7},{6,8},{7,9},{8,10},{9,11},{10,... | collective-permute-start | bytes 589832 | tf_op jit(solution)/shard_map/ppermute | solution.py:38
  76.0 3.4 %collective-permute-start.15 = (bf16[1024,256]{1,0:T(8,128)(2,1)S(1)}, bf16[1024,256]{1,0:T(8,128)(2,1)S(1)}, u32[]{:S(2)}, u32[]{:S(2)}) collective-permute-start(bf16[1024,256]{1,0:T(8,128)(2,1)S(1)} %add_convert_fusion.3), channel_id=1, source_target_pairs={{0,16},{16,0},{32,48},{48,32},{64,80},{80,64},{96,112},{112,96},{1... | collective-permute-start | bytes 1572872 | tf_op jit(solution)/shard_map/ppermute | solution.py:42
  92.1 6.4 %collective-permute-start.16 = (bf16[128,256]{1,0:T(8,128)(2,1)S(1)}, bf16[128,256]{1,0:T(8,128)(2,1)S(1)}, u32[]{:S(2)}, u32[]{:S(2)}) collective-permute-start(bf16[128,256]{1,0:T(8,128)(2,1)S(1)} %get-tuple-element.7), channel_id=1, source_target_pairs={{0,10},{1,11},{2,12},{3,13},{4,14},{5,15},{6,0},{7,1},{8,2},{9,3},... | collective-permute-start | bytes 196616 | tf_op jit(solution)/shard_map/ppermute | solution.py:38
  92.4 6.0 %collective-permute-start.17 = (bf16[128,256]{1,0:T(8,128)(2,1)S(1)}, bf16[128,256]{1,0:T(8,128)(2,1)S(1)}, u32[]{:S(2)}, u32[]{:S(2)}) collective-permute-start(bf16[128,256]{1,0:T(8,128)(2,1)S(1)} %get-tuple-element.7), channel_id=1, source_target_pairs={{0,4},{1,5},{2,6},{3,7},{4,8},{5,9},{6,10},{7,11},{8,12},{9,13},{1... | collective-permute-start | bytes 196616 | tf_op jit(solution)/shard_map/ppermute | solution.py:38
  98.5 6.6 %collective-permute-start.18 = (bf16[384,256]{1,0:T(8,128)(2,1)S(1)}, bf16[384,256]{1,0:T(8,128)(2,1)S(1)}, u32[]{:S(2)}, u32[]{:S(2)}) collective-permute-start(bf16[384,256]{1,0:T(8,128)(2,1)S(1)} %pad_maximum_fusion.1), channel_id=1, source_target_pairs={{0,1},{1,0},{2,3},{3,2},{4,5},{5,4},{6,7},{7,6},{8,9},{9,8},{10,11... | collective-permute-start | bytes 589832 | tf_op jit(solution)/shard_map/ppermute | solution.py:38
  101.0 8.6 %collective-permute-start.19 = (bf16[384,256]{1,0:T(8,128)(2,1)S(1)}, bf16[384,256]{1,0:T(8,128)(2,1)S(1)}, u32[]{:S(2)}, u32[]{:S(2)}) collective-permute-start(bf16[384,256]{1,0:T(8,128)(2,1)S(1)} %pad_maximum_fusion.1), channel_id=1, source_target_pairs={{0,2},{1,3},{2,4},{3,5},{4,6},{5,7},{6,8},{7,9},{8,10},{9,11},{10,... | collective-permute-start | bytes 589832 | tf_op jit(solution)/shard_map/ppermute | solution.py:38
  104.6 5.9 %collective-permute-start.20 = (bf16[256,256]{1,0:T(8,128)(2,1)S(1)}, bf16[256,256]{1,0:T(8,128)(2,1)S(1)}, u32[]{:S(2)}, u32[]{:S(2)}) collective-permute-start(bf16[256,256]{1,0:T(8,128)(2,1)S(1)} %pad_maximum_fusion.5), channel_id=1, source_target_pairs={{0,14},{1,15},{2,0},{3,1},{4,2},{5,3},{6,4},{7,5},{8,6},{9,7},{10,... | collective-permute-start | bytes 393224 | tf_op jit(solution)/shard_map/ppermute | solution.py:38
  105.1 10.6 %collective-permute-start.22 = (bf16[256,256]{1,0:T(8,128)(2,1)S(1)}, bf16[256,256]{1,0:T(8,128)(2,1)S(1)}, u32[]{:S(2)}, u32[]{:S(2)}) collective-permute-start(bf16[256,256]{1,0:T(8,128)(2,1)S(1)} %slice.58), channel_id=1, source_target_pairs={{0,14},{1,15},{2,0},{3,1},{4,2},{5,3},{6,4},{7,5},{8,6},{9,7},{10,... | collective-permute-start | bytes 393224 | tf_op jit(solution)/shard_map/ppermute | solution.py:38
  109.5 6.1 %collective-permute-start.21 = (bf16[384,256]{1,0:T(8,128)(2,1)S(1)}, bf16[384,256]{1,0:T(8,128)(2,1)S(1)}, u32[]{:S(2)}, u32[]{:S(2)}) collective-permute-start(bf16[384,256]{1,0:T(8,128)(2,1)S(1)} %collective-permute-done.18), channel_id=1, source_target_pairs={{0,2},{1,3},{2,4},{3,5},{4,6},{5,7},{6,8},{7,9},{8,10},{9,11},{10,... | collective-permute-start | bytes 589832 | tf_op jit(solution)/shard_map/ppermute | solution.py:38
  116.4 4.3 %collective-permute-start.23 = (bf16[1024,256]{1,0:T(8,128)(2,1)S(1)}, bf16[1024,256]{1,0:T(8,128)(2,1)S(1)}, u32[]{:S(2)}, u32[]{:S(2)}) collective-permute-start(bf16[1024,256]{1,0:T(8,128)(2,1)S(1)} %add_convert_fusion.1), channel_id=1, source_target_pairs={{0,16},{16,0},{32,48},{48,32},{64,80},{80,64},{96,112},{112,96},{1... | collective-permute-start | bytes 1572872 | tf_op jit(solution)/shard_map/ppermute | solution.py:42

commit v2 on v0

--- a/solution.py
+++ b/solution.py
@@ -15,16 +15,9 @@
 NY, NX, NZ = 4, 2, 8
 YX_GROUPS = [[2 * i + c for i in range(NY * NX)] for c in range(2)]
 ARRIVAL = [
-    (o, f)
-    for f, offsets in (
-        (0, (0, 3, -2)),
-        (1, (0, 3, -2)),
-        (0, (-1, 2, -3)),
-        (0, (1, 4)),
-        (1, (-1, 2, -3)),
-        (1, (1, 4)),
-    )
-    for o in offsets
+    (0, 0), (0, 1), (3, 0), (-2, 0), (3, 1), (-2, 1),
+    (-1, 0), (-1, 1), (2, 0), (-3, 0), (1, 0), (1, 1), (4, 0),
+    (2, 1), (-3, 1), (4, 1),
 ]
 
 
@@ -98,15 +91,15 @@
 
 
 def far_phase(h):
-    return shift_dst(h, -3), shift_dst(h, 2)
+    return shift_dst(h, 0, 1), shift_dst(h, -3), shift_dst(h, 2)
 
 
-def gather_dst(h, low, high):
-    g = jnp.concatenate([h, low, high])
-    x = shift_dst(g, 0, 1)
-    up, down = shift_dst(g, 1), shift_dst(g[: 2 * BS], -1)
-    early = jnp.concatenate([g, x, up, down])
-    late = jnp.concatenate([shift_dst(x, 1), shift_dst(x[: 2 * BS], -1)])
+def gather_dst(h, pair, low, high):
+    x = shift_dst(jnp.concatenate([low, high]), 0, 1)
+    q = jnp.concatenate([h, pair, low, high])
+    up, down = shift_dst(q, 1), shift_dst(q[: 3 * BS], -1)
+    early = jnp.concatenate([q, x, up, down])
+    late = jnp.concatenate([shift_dst(x, 1), shift_dst(x[:BS], -1)])
     return early, late
 
 
@@ -116,13 +109,13 @@
 
     s, d = lax.axis_index("src"), lax.axis_index("dst")
     info = jnp.concatenate([jnp.stack([s % 2, d // 2, d % 2]).astype(jnp.int32), block_cols])
-    low, high = far_phase(encoded)
+    far = far_phase(encoded)
     other_rows, own = pack(block_weights, info, 1, encoded)
     (own_rows,) = pack(block_weights, info, 0)
 
     kept = []
     for step in range(HOPS):
-        near, rest = gather_dst(own, low, high)
+        near, rest = gather_dst(own, *far)
         n = near.shape[0]
 
         def early(a):
@@ -143,7 +136,7 @@
         own = normalize_rows(total)
         kept.append(own)
         if step < HOPS - 1:
-            low, high = far_phase(own)
+            far = far_phase(own)
     return (encoded, jnp.stack(kept))
 
 

time: 133 us -> 131 us (0.985)
  waiting for transfers between devices: 25.7 us -> 22.1 us
  starting transfers between devices: 45.5 us -> 48 us
    ppermute x21 -> x24, waiting for transfers between devices: 25.7 us -> 22.1 us  [shift_dst(): return lax.ppermute(x, 'dst', perm)]
    ppermute x21 -> x24, starting transfers between devices: 33.4 us -> 36 us  [shift_dst(): return lax.ppermute(x, 'dst', perm)]
    unnamed x23 -> x27, local copies, waits for them, and re-layouts: 4.51 us -> 4.51 us
  transfers between devices with their start and end apart: 24 -> 27, of which waited for: 10 -> 12; matrix products, arithmetic and copies ran while one was open for 7% -> 7% of each run, Pallas kernels for 2% -> 2%
where the time goes in v2:
time: 131 us
  starting transfers between devices  48 us (37%)
  blocking collectives  37.8 us (29%)
  waiting for transfers between devices  22.1 us (17%)
  matrix products  10.8 us (8%)
  local copies, waits for them, and re-layouts  4.59 us (4%)
  other arithmetic  3.69 us (3%)
  Pallas kernels  2.78 us (2%)
    all_to_all x3, blocking collectives, shards(): lax.all_to_all(mine.astype(BF).reshape(NY * NX, BS, -1), 'src', 0, 0, axi...  37.8 us
    ppermute x24, starting transfers between devices, shift_dst(): return lax.ppermute(x, 'dst', perm)  36 us
    ppermute x24, waiting for transfers between devices, shift_dst(): return lax.ppermute(x, 'dst', perm)  22.1 us
    ppermute x3, starting transfers between devices, swap_core(): return lax.ppermute(x, 'src', [(i, i ^ 1) for i in range(NY * NX * 2)])  12 us
    dot_general x6, matrix products, early(): jnp.dot(a[:, :n], near, preferred_element_type=F32)  6.79 us
    unnamed x27, local copies, waits for them, and re-layouts  4.51 us
    pallas_call x2, Pallas kernels, pack(): pl.pallas_call(functools.partial(pack_kernel, other), out_shape=[jax.Shap...  2.78 us
  transfers between devices with their start and end apart: 27, of which 12 were waited for; matrix products, arithmetic and copies ran while one was open for 7% of the time, Pallas kernels for 2%

profile of v2, /device:TPU:1, one launch (start us, length us, event | category | flops | bytes accessed | tf_op | source)
XLA Modules:
  0.0 130.9 jit_solution(15080587936321310663)
XLA Ops:
  0.6 0.9 copy-done
  1.6 1.4 %multiply_reduce_fusion.2 = (f32[128]{0:T(128)S(1)}, f32[128,256]{1,0:T(8,128)S(1)}) fusion(bf16[512,256]{1,0:T(8,128)(2,1)S(1)} %copy-done, bf16[128,256]{1,0:T(8,128)(2,1)} %param.6, bf16[256,512]{1,0:T(8,128)(2,1)} %param.7), kind=kOutput, calls=%fused_computation.66 | convolution fusion | flops 67501952 | bytes 721408 | tf_op jit(solution)/shard_map/dot_general | solution.py:108
  3.1 3.7 %collective-permute-start = (bf16[128,256]{1,0:T(8,128)(2,1)S(1)}, bf16[128,256]{1,0:T(8,128)(2,1)S(1)}, u32[]{:S(2)}, u32[]{:S(2)}) collective-permute-start(bf16[128,256]{1,0:T(8,128)(2,1)S(1)} %multiply_convert_fusion.3.refs_0_), channel_id=1, source_target_pairs={{0,1},{1,0},{2,3},{3,2},{4,5},{5,4},{6,7},{7,6},{8,9},{9,8},{10,11... | collective-permute-start | bytes 196616 | tf_op jit(solution)/shard_map/ppermute | solution.py:26
  6.8 6.5 %collective-permute-start.1 = (bf16[128,256]{1,0:T(8,128)(2,1)S(1)}, bf16[128,256]{1,0:T(8,128)(2,1)S(1)}, u32[]{:S(2)}, u32[]{:S(2)}) collective-permute-start(bf16[128,256]{1,0:T(8,128)(2,1)S(1)} %multiply_convert_fusion.3.refs_0_), channel_id=1, source_target_pairs={{0,10},{1,11},{2,12},{3,13},{4,14},{5,15},{6,0},{7,1},{8,2},{9,3},... | collective-permute-start | bytes 196616 | tf_op jit(solution)/shard_map/ppermute | solution.py:26
  13.3 1.2 collective-permute-start.2
  14.4 0.7 pad_add_fusion.info_ref
  15.2 3.4 %copy-done.1 = f32[128,128,128]{2,1,0:T(8,128)S(1)} copy-done((f32[128,128,128]{2,1,0:T(8,128)S(1)}, f32[128,128,128]{2,1,0:T(8,128)}, u32[]{:S(2)}) %copy-start.1) | copy-done | bytes 8388632
  18.6 1.4 %pack.3 = (bf16[1024,2048]{1,0:T(8,128)(2,1)S(1)}, bf16[128,256]{1,0:T(8,128)(2,1)S(1)}) custom-call(s32[131]{0:T(256)S(1)} %pad_add_fusion.info_ref, f32[8,2,8,128,128]{4,3,2,1,0:T(8,128)S(1)} %bitcast.54, bf16[128,256]{1,0:T(8,128)(2,1)S(1)} %multiply_convert_fusion.3.refs_0_), custom_call_target="tpu_custom_call" | custom-call | bytes 6291456 | tf_op jit(solution)/shard_map/pack/pallas_call | solution.py:74
  20.0 1.4 %pack.2 = bf16[1024,2048]{1,0:T(8,128)(2,1)S(1)} custom-call(s32[131]{0:T(256)S(1)} %pad_add_fusion.info_ref, f32[8,2,8,128,128]{4,3,2,1,0:T(8,128)S(1)} %bitcast.55), custom_call_target="tpu_custom_call" | custom-call | bytes 6291456 | tf_op jit(solution)/shard_map/pack/pallas_call | solution.py:74
  21.4 0.3 collective-permute-start.3
  21.9 2.7 %collective-permute-start.5 = (bf16[384,256]{1,0:T(8,128)(2,1)S(1)}, bf16[384,256]{1,0:T(8,128)(2,1)S(1)}, u32[]{:S(2)}, u32[]{:S(2)}) collective-permute-start(bf16[384,256]{1,0:T(8,128)(2,1)S(1)} %pad_maximum_fusion.3), channel_id=1, source_target_pairs={{0,14},{1,15},{2,0},{3,1},{4,2},{5,3},{6,4},{7,5},{8,6},{9,7},{10,... | collective-permute-start | bytes 589832 | tf_op jit(solution)/shard_map/ppermute | solution.py:26
  24.7 2.2 %collective-permute-done.3 = bf16[256,256]{1,0:T(8,128)(2,1)S(1)} collective-permute-done((bf16[256,256]{1,0:T(8,128)(2,1)S(1)}, bf16[256,256]{1,0:T(8,128)(2,1)S(1)}, u32[]{:S(2)}, u32[]{:S(2)}) %collective-permute-start.3) | collective-permute-done | bytes 131104 | tf_op jit(solution)/shard_map/ppermute | solution.py:26
  26.8 1.9 %collective-permute-start.7 = (bf16[128,256]{1,0:T(8,128)(2,1)S(1)}, bf16[128,256]{1,0:T(8,128)(2,1)S(1)}, u32[]{:S(2)}, u32[]{:S(2)}) collective-permute-start(bf16[128,256]{1,0:T(8,128)(2,1)S(1)} %slice.56), channel_id=1, source_target_pairs={{0,14},{1,15},{2,0},{3,1},{4,2},{5,3},{6,4},{7,5},{8,6},{9,7},{10,... | collective-permute-start | bytes 196616 | tf_op jit(solution)/shard_map/ppermute | solution.py:26
  28.8 0.3 collective-permute-done.4
  29.1 1.1 fusion.10
  30.3 3.5 %collective-permute-done.6 = bf16[256,256]{1,0:T(8,128)(2,1)S(1)} collective-permute-done((bf16[256,256]{1,0:T(8,128)(2,1)S(1)}, bf16[256,256]{1,0:T(8,128)(2,1)S(1)}, u32[]{:S(2)}, u32[]{:S(2)}) %collective-permute-start.6) | collective-permute-done | bytes 131104 | tf_op jit(solution)/shard_map/ppermute | solution.py:26
  33.8 0.4 fusion.22
  34.3 0.2 add_convert_fusion.5
  34.5 4.2 %collective-permute-start.8 = (bf16[1024,256]{1,0:T(8,128)(2,1)S(1)}, bf16[1024,256]{1,0:T(8,128)(2,1)S(1)}, u32[]{:S(2)}, u32[]{:S(2)}) collective-permute-start(bf16[1024,256]{1,0:T(8,128)(2,1)S(1)} %add_convert_fusion.5), channel_id=1, source_target_pairs={{0,16},{16,0},{32,48},{48,32},{64,80},{80,64},{96,112},{112,96},{1... | collective-permute-start | bytes 1572872 | tf_op jit(solution)/shard_map/ppermute | solution.py:30
  38.6 1.1 fusion.4
  39.8 0.4 fusion.16
  40.2 0.2 add_convert_fusion.4
  40.4 13.3 %all_to_all.15 = bf16[8,128,256]{2,1,0:T(8,128)(2,1)S(1)} all-to-all(bf16[8,128,256]{2,1,0:T(8,128)(2,1)S(1)} %bitcast.56), channel_id=1, replica_groups={{0,32,64,96,128,160,192,224},{16,48,80,112,144,176,208,240},{1,33,65,97..., dimensions={0} | all-to-all | bytes 1048576 | tf_op jit(solution)/shard_map/all_to_all | solution.py:132
  54.2 1.6 %collective-permute-start.11 = (bf16[128,256]{1,0:T(8,128)(2,1)S(1)}, bf16[128,256]{1,0:T(8,128)(2,1)S(1)}, u32[]{:S(2)}, u32[]{:S(2)}) collective-permute-start(bf16[128,256]{1,0:T(8,128)(2,1)S(1)} %get-tuple-element.9), channel_id=1, source_target_pairs={{0,4},{1,5},{2,6},{3,7},{4,8},{5,9},{6,10},{7,11},{8,12},{9,13},{1... | collective-permute-start | bytes 196616 | tf_op jit(solution)/shard_map/ppermute | solution.py:26
  55.7 1.7 %collective-permute-start.9 = (bf16[128,256]{1,0:T(8,128)(2,1)S(1)}, bf16[128,256]{1,0:T(8,128)(2,1)S(1)}, u32[]{:S(2)}, u32[]{:S(2)}) collective-permute-start(bf16[128,256]{1,0:T(8,128)(2,1)S(1)} %get-tuple-element.9), channel_id=1, source_target_pairs={{0,1},{1,0},{2,3},{3,2},{4,5},{5,4},{6,7},{7,6},{8,9},{9,8},{10,11... | collective-permute-start | bytes 196616 | tf_op jit(solution)/shard_map/ppermute | solution.py:26
  57.5 2.4 %collective-permute-done.10 = bf16[128,256]{1,0:T(8,128)(2,1)S(1)} collective-permute-done((bf16[128,256]{1,0:T(8,128)(2,1)S(1)}, bf16[128,256]{1,0:T(8,128)(2,1)S(1)}, u32[]{:S(2)}, u32[]{:S(2)}) %collective-permute-start.10) | collective-permute-done | bytes 65568 | tf_op jit(solution)/shard_map/ppermute | solution.py:26
  59.9 1.8 %collective-permute-start.12 = (bf16[256,256]{1,0:T(8,128)(2,1)S(1)}, bf16[256,256]{1,0:T(8,128)(2,1)S(1)}, u32[]{:S(2)}, u32[]{:S(2)}) collective-permute-start(bf16[256,256]{1,0:T(8,128)(2,1)S(1)} %pad_maximum_fusion.8), channel_id=1, source_target_pairs={{0,1},{1,0},{2,3},{3,2},{4,5},{5,4},{6,7},{7,6},{8,9},{9,8},{10,11... | collective-permute-start | bytes 393224 | tf_op jit(solution)/shard_map/ppermute | solution.py:26
  61.8 0.7 collective-permute-start.13
  62.5 2.1 %collective-permute-start.14 = (bf16[384,256]{1,0:T(8,128)(2,1)S(1)}, bf16[384,256]{1,0:T(8,128)(2,1)S(1)}, u32[]{:S(2)}, u32[]{:S(2)}) collective-permute-start(bf16[384,256]{1,0:T(8,128)(2,1)S(1)} %pad_maximum_fusion.4), channel_id=1, source_target_pairs={{0,14},{1,15},{2,0},{3,1},{4,2},{5,3},{6,4},{7,5},{8,6},{9,7},{10,... | collective-permute-start | bytes 589832 | tf_op jit(solution)/shard_map/ppermute | solution.py:26
  64.7 0.7 collective-permute-done.12
  65.4 0.2 collective-permute-start.16
  65.6 1.3 collective-permute-start.15
  66.8 1.8 %collective-permute-done.13 = bf16[512,256]{1,0:T(8,128)(2,1)S(1)} collective-permute-done((bf16[512,256]{1,0:T(8,128)(2,1)S(1)}, bf16[512,256]{1,0:T(8,128)(2,1)S(1)}, u32[]{:S(2)}, u32[]{:S(2)}) %collective-permute-start.13) | collective-permute-done | bytes 262176 | tf_op jit(solution)/shard_map/ppermute | solution.py:26
  68.7 1.1 fusion.8
  69.8 2.5 %collective-permute-done.15 = bf16[256,256]{1,0:T(8,128)(2,1)S(1)} collective-permute-done((bf16[256,256]{1,0:T(8,128)(2,1)S(1)}, bf16[256,256]{1,0:T(8,128)(2,1)S(1)}, u32[]{:S(2)}, u32[]{:S(2)}) %collective-permute-start.15) | collective-permute-done | bytes 131104 | tf_op jit(solution)/shard_map/ppermute | solution.py:26
  72.3 0.4 fusion.20
  72.8 0.2 add_convert_fusion.3
  72.9 4.4 %collective-permute-start.17 = (bf16[1024,256]{1,0:T(8,128)(2,1)S(1)}, bf16[1024,256]{1,0:T(8,128)(2,1)S(1)}, u32[]{:S(2)}, u32[]{:S(2)}) collective-permute-start(bf16[1024,256]{1,0:T(8,128)(2,1)S(1)} %add_convert_fusion.3), channel_id=1, source_target_pairs={{0,16},{16,0},{32,48},{48,32},{64,80},{80,64},{96,112},{112,96},{1... | collective-permute-start | bytes 1572872 | tf_op jit(solution)/shard_map/ppermute | solution.py:30
  77.4 1.1 fusion.2
  78.5 0.4 fusion.14
  79.0 0.2 add_convert_fusion.2
  79.2 12.3 %all_to_all.16 = bf16[8,128,256]{2,1,0:T(8,128)(2,1)S(1)} all-to-all(bf16[8,128,256]{2,1,0:T(8,128)(2,1)S(1)} %bitcast.57), channel_id=1, replica_groups={{0,32,64,96,128,160,192,224},{16,48,80,112,144,176,208,240},{1,33,65,97..., dimensions={0} | all-to-all | bytes 1048576 | tf_op jit(solution)/shard_map/all_to_all | solution.py:132
  91.8 0.3 collective-permute-start.19
  92.1 1.2 collective-permute-start.20
  93.3 1.8 %collective-permute-start.18 = (bf16[128,256]{1,0:T(8,128)(2,1)S(1)}, bf16[128,256]{1,0:T(8,128)(2,1)S(1)}, u32[]{:S(2)}, u32[]{:S(2)}) collective-permute-start(bf16[128,256]{1,0:T(8,128)(2,1)S(1)} %get-tuple-element.7), channel_id=1, source_target_pairs={{0,1},{1,0},{2,3},{3,2},{4,5},{5,4},{6,7},{7,6},{8,9},{9,8},{10,11... | collective-permute-start | bytes 196616 | tf_op jit(solution)/shard_map/ppermute | solution.py:26
  95.1 2.8 %collective-permute-done.19 = bf16[128,256]{1,0:T(8,128)(2,1)S(1)} collective-permute-done((bf16[128,256]{1,0:T(8,128)(2,1)S(1)}, bf16[128,256]{1,0:T(8,128)(2,1)S(1)}, u32[]{:S(2)}, u32[]{:S(2)}) %collective-permute-start.19) | collective-permute-done | bytes 65568 | tf_op jit(solution)/shard_map/ppermute | solution.py:26
  97.9 1.9 %collective-permute-start.21 = (bf16[256,256]{1,0:T(8,128)(2,1)S(1)}, bf16[256,256]{1,0:T(8,128)(2,1)S(1)}, u32[]{:S(2)}, u32[]{:S(2)}) collective-permute-start(bf16[256,256]{1,0:T(8,128)(2,1)S(1)} %pad_maximum_fusion.9), channel_id=1, source_target_pairs={{0,1},{1,0},{2,3},{3,2},{4,5},{5,4},{6,7},{7,6},{8,9},{9,8},{10,11... | collective-permute-start | bytes 393224 | tf_op jit(solution)/shard_map/ppermute | solution.py:26
  99.8 1.9 %collective-permute-start.22 = (bf16[512,256]{1,0:T(8,128)(2,1)S(1)}, bf16[512,256]{1,0:T(8,128)(2,1)S(1)}, u32[]{:S(2)}, u32[]{:S(2)}) collective-permute-start(bf16[512,256]{1,0:T(8,128)(2,1)S(1)} %pad_maximum_fusion.2), channel_id=1, source_target_pairs={{0,2},{1,3},{2,4},{3,5},{4,6},{5,7},{6,8},{7,9},{8,10},{9,11},{10,... | collective-permute-start | bytes 786440 | tf_op jit(solution)/shard_map/ppermute | solution.py:26
  101.8 1.1 collective-permute-start.23
  102.9 0.4 collective-permute-done.21
  103.3 1.9 %collective-permute-start.25 = (bf16[128,256]{1,0:T(8,128)(2,1)S(1)}, bf16[128,256]{1,0:T(8,128)(2,1)S(1)}, u32[]{:S(2)}, u32[]{:S(2)}) collective-permute-start(bf16[128,256]{1,0:T(8,128)(2,1)S(1)} %slice.58), channel_id=1, source_target_pairs={{0,14},{1,15},{2,0},{3,1},{4,2},{5,3},{6,4},{7,5},{8,6},{9,7},{10,... | collective-permute-start | bytes 196616 | tf_op jit(solution)/shard_map/ppermute | solution.py:26
  105.1 1.5 %collective-permute-done.22 = bf16[512,256]{1,0:T(8,128)(2,1)S(1)} collective-permute-done((bf16[512,256]{1,0:T(8,128)(2,1)S(1)}, bf16[512,256]{1,0:T(8,128)(2,1)S(1)}, u32[]{:S(2)}, u32[]{:S(2)}) %collective-permute-start.22) | collective-permute-done | bytes 262176 | tf_op jit(solution)/shard_map/ppermute | solution.py:26
  106.6 0.2 collective-permute-done.23
  106.9 1.1 fusion.6
  108.0 3.9 %collective-permute-done.24 = bf16[256,256]{1,0:T(8,128)(2,1)S(1)} collective-permute-done((bf16[256,256]{1,0:T(8,128)(2,1)S(1)}, bf16[256,256]{1,0:T(8,128)(2,1)S(1)}, u32[]{:S(2)}, u32[]{:S(2)}) %collective-permute-start.24) | collective-permute-done | bytes 131104 | tf_op jit(solution)/shard_map/ppermute | solution.py:26
  111.9 0.4 fusion.18
  112.4 0.2 add_convert_fusion.1
  112.5 3.3 %collective-permute-start.26 = (bf16[1024,256]{1,0:T(8,128)(2,1)S(1)}, bf16[1024,256]{1,0:T(8,128)(2,1)S(1)}, u32[]{:S(2)}, u32[]{:S(2)}) collective-permute-start(bf16[1024,256]{1,0:T(8,128)(2,1)S(1)} %add_convert_fusion.1), channel_id=1, source_target_pairs={{0,16},{16,0},{32,48},{48,32},{64,80},{80,64},{96,112},{112,96},{1... | collective-permute-start | bytes 1572872 | tf_op jit(solution)/shard_map/ppermute | solution.py:30
  115.9 1.1 fusion
  117.0 0.4 fusion.12
  117.5 0.2 add_convert_fusion
  117.7 12.2 %all_to_all.17 = bf16[8,128,256]{2,1,0:T(8,128)(2,1)S(1)} all-to-all(bf16[8,128,256]{2,1,0:T(8,128)(2,1)S(1)} %bitcast.58), channel_id=1, replica_groups={{0,32,64,96,128,160,192,224},{16,48,80,112,144,176,208,240},{1,33,65,97..., dimensions={0} | all-to-all | bytes 1048576 | tf_op jit(solution)/shard_map/all_to_all | solution.py:132
  130.1 0.1 fusion.25
  130.2 0.7 pad_maximum_fusion.6
  (75 shorter events, 1.5 us)
Async XLA Ops:
  0.6 1.0 copy-start
  3.1 16.9 %copy-start.2 = (bf16[128,256]{1,0:T(8,128)(2,1)}, bf16[128,256]{1,0:T(8,128)(2,1)S(1)}, u32[]{:S(2)}) copy-start(bf16[128,256]{1,0:T(8,128)(2,1)S(1)} %multiply_convert_fusion.3.refs_0_) | copy-start | bytes 196612
  3.1 18.6 %collective-permute-start = (bf16[128,256]{1,0:T(8,128)(2,1)S(1)}, bf16[128,256]{1,0:T(8,128)(2,1)S(1)}, u32[]{:S(2)}, u32[]{:S(2)}) collective-permute-start(bf16[128,256]{1,0:T(8,128)(2,1)S(1)} %multiply_convert_fusion.3.refs_0_), channel_id=1, source_target_pairs={{0,1},{1,0},{2,3},{3,2},{4,5},{5,4},{6,7},{7,6},{8,9},{9,8},{10,11... | collective-permute-start | bytes 196616 | tf_op jit(solution)/shard_map/ppermute | solution.py:26
  6.8 14.6 %collective-permute-start.1 = (bf16[128,256]{1,0:T(8,128)(2,1)S(1)}, bf16[128,256]{1,0:T(8,128)(2,1)S(1)}, u32[]{:S(2)}, u32[]{:S(2)}) collective-permute-start(bf16[128,256]{1,0:T(8,128)(2,1)S(1)} %multiply_convert_fusion.3.refs_0_), channel_id=1, source_target_pairs={{0,10},{1,11},{2,12},{3,13},{4,14},{5,15},{6,0},{7,1},{8,2},{9,3},... | collective-permute-start | bytes 196616 | tf_op jit(solution)/shard_map/ppermute | solution.py:26
  13.3 8.1 %collective-permute-start.2 = (bf16[128,256]{1,0:T(8,128)(2,1)S(1)}, bf16[128,256]{1,0:T(8,128)(2,1)S(1)}, u32[]{:S(2)}, u32[]{:S(2)}) collective-permute-start(bf16[128,256]{1,0:T(8,128)(2,1)S(1)} %multiply_convert_fusion.3.refs_0_), channel_id=1, source_target_pairs={{0,4},{1,5},{2,6},{3,7},{4,8},{5,9},{6,10},{7,11},{8,12},{9,13},{1... | collective-permute-start | bytes 196616 | tf_op jit(solution)/shard_map/ppermute | solution.py:26
  15.2 3.4 %copy-start.1 = (f32[128,128,128]{2,1,0:T(8,128)S(1)}, f32[128,128,128]{2,1,0:T(8,128)}, u32[]{:S(2)}) copy-start(f32[128,128,128]{2,1,0:T(8,128)} %param.9) | copy-start | bytes 25165828
  21.4 5.4 %collective-permute-start.3 = (bf16[256,256]{1,0:T(8,128)(2,1)S(1)}, bf16[256,256]{1,0:T(8,128)(2,1)S(1)}, u32[]{:S(2)}, u32[]{:S(2)}) collective-permute-start(bf16[256,256]{1,0:T(8,128)(2,1)S(1)} %pad_maximum_fusion.7), channel_id=1, source_target_pairs={{0,1},{1,0},{2,3},{3,2},{4,5},{5,4},{6,7},{7,6},{8,9},{9,8},{10,11... | collective-permute-start | bytes 393224 | tf_op jit(solution)/shard_map/ppermute | solution.py:26
  21.8 7.3 %collective-permute-start.4 = (bf16[512,256]{1,0:T(8,128)(2,1)S(1)}, bf16[512,256]{1,0:T(8,128)(2,1)S(1)}, u32[]{:S(2)}, u32[]{:S(2)}) collective-permute-start(bf16[512,256]{1,0:T(8,128)(2,1)S(1)} %pad_maximum_fusion), channel_id=1, source_target_pairs={{0,2},{1,3},{2,4},{3,5},{4,6},{5,7},{6,8},{7,9},{8,10},{9,11},{10,... | collective-permute-start | bytes 786440 | tf_op jit(solution)/shard_map/ppermute | solution.py:26
  21.9 7.2 %collective-permute-start.5 = (bf16[384,256]{1,0:T(8,128)(2,1)S(1)}, bf16[384,256]{1,0:T(8,128)(2,1)S(1)}, u32[]{:S(2)}, u32[]{:S(2)}) collective-permute-start(bf16[384,256]{1,0:T(8,128)(2,1)S(1)} %pad_maximum_fusion.3), channel_id=1, source_target_pairs={{0,14},{1,15},{2,0},{3,1},{4,2},{5,3},{6,4},{7,5},{8,6},{9,7},{10,... | collective-permute-start | bytes 589832 | tf_op jit(solution)/shard_map/ppermute | solution.py:26
  26.8 7.0 %collective-permute-start.7 = (bf16[128,256]{1,0:T(8,128)(2,1)S(1)}, bf16[128,256]{1,0:T(8,128)(2,1)S(1)}, u32[]{:S(2)}, u32[]{:S(2)}) collective-permute-start(bf16[128,256]{1,0:T(8,128)(2,1)S(1)} %slice.56), channel_id=1, source_target_pairs={{0,14},{1,15},{2,0},{3,1},{4,2},{5,3},{6,4},{7,5},{8,6},{9,7},{10,... | collective-permute-start | bytes 196616 | tf_op jit(solution)/shard_map/ppermute | solution.py:26
  28.8 5.0 %collective-permute-start.6 = (bf16[256,256]{1,0:T(8,128)(2,1)S(1)}, bf16[256,256]{1,0:T(8,128)(2,1)S(1)}, u32[]{:S(2)}, u32[]{:S(2)}) collective-permute-start(bf16[256,256]{1,0:T(8,128)(2,1)S(1)} %collective-permute-done.3), channel_id=1, source_target_pairs={{0,2},{1,3},{2,4},{3,5},{4,6},{5,7},{6,8},{7,9},{8,10},{9,11},{10,... | collective-permute-start | bytes 393224 | tf_op jit(solution)/shard_map/ppermute | solution.py:26
  34.5 5.8 %collective-permute-start.8 = (bf16[1024,256]{1,0:T(8,128)(2,1)S(1)}, bf16[1024,256]{1,0:T(8,128)(2,1)S(1)}, u32[]{:S(2)}, u32[]{:S(2)}) collective-permute-start(bf16[1024,256]{1,0:T(8,128)(2,1)S(1)} %add_convert_fusion.5), channel_id=1, source_target_pairs={{0,16},{16,0},{32,48},{48,32},{64,80},{80,64},{96,112},{112,96},{1... | collective-permute-start | bytes 1572872 | tf_op jit(solution)/shard_map/ppermute | solution.py:30
  39.8 14.0 %copy-start.3 = (bf16[3,128,256]{2,1,0:T(8,128)(2,1)S(1)}, bf16[3,128,256]{2,1,0:T(8,128)(2,1)}, u32[]{:S(2)}) copy-start(bf16[3,128,256]{2,1,0:T(8,128)(2,1)} %param.11) | copy-start | bytes 589828
  54.1 5.9 %collective-permute-start.10 = (bf16[128,256]{1,0:T(8,128)(2,1)S(1)}, bf16[128,256]{1,0:T(8,128)(2,1)S(1)}, u32[]{:S(2)}, u32[]{:S(2)}) collective-permute-start(bf16[128,256]{1,0:T(8,128)(2,1)S(1)} %get-tuple-element.9), channel_id=1, source_target_pairs={{0,10},{1,11},{2,12},{3,13},{4,14},{5,15},{6,0},{7,1},{8,2},{9,3},... | collective-permute-start | bytes 196616 | tf_op jit(solution)/shard_map/ppermute | solution.py:26
  54.2 5.8 %collective-permute-start.11 = (bf16[128,256]{1,0:T(8,128)(2,1)S(1)}, bf16[128,256]{1,0:T(8,128)(2,1)S(1)}, u32[]{:S(2)}, u32[]{:S(2)}) collective-permute-start(bf16[128,256]{1,0:T(8,128)(2,1)S(1)} %get-tuple-element.9), channel_id=1, source_target_pairs={{0,4},{1,5},{2,6},{3,7},{4,8},{5,9},{6,10},{7,11},{8,12},{9,13},{1... | collective-permute-start | bytes 196616 | tf_op jit(solution)/shard_map/ppermute | solution.py:26
  55.7 6.0 %collective-permute-start.9 = (bf16[128,256]{1,0:T(8,128)(2,1)S(1)}, bf16[128,256]{1,0:T(8,128)(2,1)S(1)}, u32[]{:S(2)}, u32[]{:S(2)}) collective-permute-start(bf16[128,256]{1,0:T(8,128)(2,1)S(1)} %get-tuple-element.9), channel_id=1, source_target_pairs={{0,1},{1,0},{2,3},{3,2},{4,5},{5,4},{6,7},{7,6},{8,9},{9,8},{10,11... | collective-permute-start | bytes 196616 | tf_op jit(solution)/shard_map/ppermute | solution.py:26
  59.9 5.4 %collective-permute-start.12 = (bf16[256,256]{1,0:T(8,128)(2,1)S(1)}, bf16[256,256]{1,0:T(8,128)(2,1)S(1)}, u32[]{:S(2)}, u32[]{:S(2)}) collective-permute-start(bf16[256,256]{1,0:T(8,128)(2,1)S(1)} %pad_maximum_fusion.8), channel_id=1, source_target_pairs={{0,1},{1,0},{2,3},{3,2},{4,5},{5,4},{6,7},{7,6},{8,9},{9,8},{10,11... | collective-permute-start | bytes 393224 | tf_op jit(solution)/shard_map/ppermute | solution.py:26
  61.8 6.8 %collective-permute-start.13 = (bf16[512,256]{1,0:T(8,128)(2,1)S(1)}, bf16[512,256]{1,0:T(8,128)(2,1)S(1)}, u32[]{:S(2)}, u32[]{:S(2)}) collective-permute-start(bf16[512,256]{1,0:T(8,128)(2,1)S(1)} %pad_maximum_fusion.1), channel_id=1, source_target_pairs={{0,2},{1,3},{2,4},{3,5},{4,6},{5,7},{6,8},{7,9},{8,10},{9,11},{10,... | collective-permute-start | bytes 786440 | tf_op jit(solution)/shard_map/ppermute | solution.py:26
  62.5 6.1 %collective-permute-start.14 = (bf16[384,256]{1,0:T(8,128)(2,1)S(1)}, bf16[384,256]{1,0:T(8,128)(2,1)S(1)}, u32[]{:S(2)}, u32[]{:S(2)}) collective-permute-start(bf16[384,256]{1,0:T(8,128)(2,1)S(1)} %pad_maximum_fusion.4), channel_id=1, source_target_pairs={{0,14},{1,15},{2,0},{3,1},{4,2},{5,3},{6,4},{7,5},{8,6},{9,7},{10,... | collective-permute-start | bytes 589832 | tf_op jit(solution)/shard_map/ppermute | solution.py:26
  65.4 6.9 %collective-permute-start.16 = (bf16[128,256]{1,0:T(8,128)(2,1)S(1)}, bf16[128,256]{1,0:T(8,128)(2,1)S(1)}, u32[]{:S(2)}, u32[]{:S(2)}) collective-permute-start(bf16[128,256]{1,0:T(8,128)(2,1)S(1)} %slice.57), channel_id=1, source_target_pairs={{0,14},{1,15},{2,0},{3,1},{4,2},{5,3},{6,4},{7,5},{8,6},{9,7},{10,... | collective-permute-start | bytes 196616 | tf_op jit(solution)/shard_map/ppermute | solution.py:26
  65.6 6.7 %collective-permute-start.15 = (bf16[256,256]{1,0:T(8,128)(2,1)S(1)}, bf16[256,256]{1,0:T(8,128)(2,1)S(1)}, u32[]{:S(2)}, u32[]{:S(2)}) collective-permute-start(bf16[256,256]{1,0:T(8,128)(2,1)S(1)} %collective-permute-done.12), channel_id=1, source_target_pairs={{0,2},{1,3},{2,4},{3,5},{4,6},{5,7},{6,8},{7,9},{8,10},{9,11},{10,... | collective-permute-start | bytes 393224 | tf_op jit(solution)/shard_map/ppermute | solution.py:26
  72.9 6.0 %collective-permute-start.17 = (bf16[1024,256]{1,0:T(8,128)(2,1)S(1)}, bf16[1024,256]{1,0:T(8,128)(2,1)S(1)}, u32[]{:S(2)}, u32[]{:S(2)}) collective-permute-start(bf16[1024,256]{1,0:T(8,128)(2,1)S(1)} %add_convert_fusion.3), channel_id=1, source_target_pairs={{0,16},{16,0},{32,48},{48,32},{64,80},{80,64},{96,112},{112,96},{1... | collective-permute-start | bytes 1572872 | tf_op jit(solution)/shard_map/ppermute | solution.py:30
  91.8 6.0 %collective-permute-start.19 = (bf16[128,256]{1,0:T(8,128)(2,1)S(1)}, bf16[128,256]{1,0:T(8,128)(2,1)S(1)}, u32[]{:S(2)}, u32[]{:S(2)}) collective-permute-start(bf16[128,256]{1,0:T(8,128)(2,1)S(1)} %get-tuple-element.7), channel_id=1, source_target_pairs={{0,10},{1,11},{2,12},{3,13},{4,14},{5,15},{6,0},{7,1},{8,2},{9,3},... | collective-permute-start | bytes 196616 | tf_op jit(solution)/shard_map/ppermute | solution.py:26
  92.1 5.7 %collective-permute-start.20 = (bf16[128,256]{1,0:T(8,128)(2,1)S(1)}, bf16[128,256]{1,0:T(8,128)(2,1)S(1)}, u32[]{:S(2)}, u32[]{:S(2)}) collective-permute-start(bf16[128,256]{1,0:T(8,128)(2,1)S(1)} %get-tuple-element.7), channel_id=1, source_target_pairs={{0,4},{1,5},{2,6},{3,7},{4,8},{5,9},{6,10},{7,11},{8,12},{9,13},{1... | collective-permute-start | bytes 196616 | tf_op jit(solution)/shard_map/ppermute | solution.py:26
  93.3 6.5 %collective-permute-start.18 = (bf16[128,256]{1,0:T(8,128)(2,1)S(1)}, bf16[128,256]{1,0:T(8,128)(2,1)S(1)}, u32[]{:S(2)}, u32[]{:S(2)}) collective-permute-start(bf16[128,256]{1,0:T(8,128)(2,1)S(1)} %get-tuple-element.7), channel_id=1, source_target_pairs={{0,1},{1,0},{2,3},{3,2},{4,5},{5,4},{6,7},{7,6},{8,9},{9,8},{10,11... | collective-permute-start | bytes 196616 | tf_op jit(solution)/shard_map/ppermute | solution.py:26
  97.9 5.4 %collective-permute-start.21 = (bf16[256,256]{1,0:T(8,128)(2,1)S(1)}, bf16[256,256]{1,0:T(8,128)(2,1)S(1)}, u32[]{:S(2)}, u32[]{:S(2)}) collective-permute-start(bf16[256,256]{1,0:T(8,128)(2,1)S(1)} %pad_maximum_fusion.9), channel_id=1, source_target_pairs={{0,1},{1,0},{2,3},{3,2},{4,5},{5,4},{6,7},{7,6},{8,9},{9,8},{10,11... | collective-permute-start | bytes 393224 | tf_op jit(solution)/shard_map/ppermute | solution.py:26
  99.8 6.8 %collective-permute-start.22 = (bf16[512,256]{1,0:T(8,128)(2,1)S(1)}, bf16[512,256]{1,0:T(8,128)(2,1)S(1)}, u32[]{:S(2)}, u32[]{:S(2)}) collective-permute-start(bf16[512,256]{1,0:T(8,128)(2,1)S(1)} %pad_maximum_fusion.2), channel_id=1, source_target_pairs={{0,2},{1,3},{2,4},{3,5},{4,6},{5,7},{6,8},{7,9},{8,10},{9,11},{10,... | collective-permute-start | bytes 786440 | tf_op jit(solution)/shard_map/ppermute | solution.py:26
  101.8 5.1 %collective-permute-start.23 = (bf16[384,256]{1,0:T(8,128)(2,1)S(1)}, bf16[384,256]{1,0:T(8,128)(2,1)S(1)}, u32[]{:S(2)}, u32[]{:S(2)}) collective-permute-start(bf16[384,256]{1,0:T(8,128)(2,1)S(1)} %pad_maximum_fusion.5), channel_id=1, source_target_pairs={{0,14},{1,15},{2,0},{3,1},{4,2},{5,3},{6,4},{7,5},{8,6},{9,7},{10,... | collective-permute-start | bytes 589832 | tf_op jit(solution)/shard_map/ppermute | solution.py:26
  103.3 8.6 %collective-permute-start.25 = (bf16[128,256]{1,0:T(8,128)(2,1)S(1)}, bf16[128,256]{1,0:T(8,128)(2,1)S(1)}, u32[]{:S(2)}, u32[]{:S(2)}) collective-permute-start(bf16[128,256]{1,0:T(8,128)(2,1)S(1)} %slice.58), channel_id=1, source_target_pairs={{0,14},{1,15},{2,0},{3,1},{4,2},{5,3},{6,4},{7,5},{8,6},{9,7},{10,... | collective-permute-start | bytes 196616 | tf_op jit(solution)/shard_map/ppermute | solution.py:26
  105.1 6.8 %collective-permute-start.24 = (bf16[256,256]{1,0:T(8,128)(2,1)S(1)}, bf16[256,256]{1,0:T(8,128)(2,1)S(1)}, u32[]{:S(2)}, u32[]{:S(2)}) collective-permute-start(bf16[256,256]{1,0:T(8,128)(2,1)S(1)} %collective-permute-done.21), channel_id=1, source_target_pairs={{0,2},{1,3},{2,4},{3,5},{4,6},{5,7},{6,8},{7,9},{8,10},{9,11},{10,... | collective-permute-start | bytes 393224 | tf_op jit(solution)/shard_map/ppermute | solution.py:26
  112.5 4.9 %collective-permute-start.26 = (bf16[1024,256]{1,0:T(8,128)(2,1)S(1)}, bf16[1024,256]{1,0:T(8,128)(2,1)S(1)}, u32[]{:S(2)}, u32[]{:S(2)}) collective-permute-start(bf16[1024,256]{1,0:T(8,128)(2,1)S(1)} %add_convert_fusion.1), channel_id=1, source_target_pairs={{0,16},{16,0},{32,48},{48,32},{64,80},{80,64},{96,112},{112,96},{1... | collective-permute-start | bytes 1572872 | tf_op jit(solution)/shard_map/ppermute | solution.py:30
